TPU v7x, 512 devices: a whole 4x4x16 slice. The times are simulated.
512 devices in a mesh: dp: 8 (over x, core), azim: 16 (over z), axial: 4 (over y).
Axes of the slice: x: 4, y: 4, z: 16, core: 2. Of those that a mesh axis runs over, the one named last changes fastest.
Arguments:
- field: bfloat16 [8, 32, 256, 8192], P('dp', None, 'azim', 'axial'), may hold values from -6 to 6
- cotangent: bfloat16 [8, 32, 256, 8192], P('dp', None, 'azim', 'axial'), may hold values from -0.119628906 to 0.119628906
- spectral_weight: bfloat16 [2, 16, 16, 16, 32, 32], P(None, 'azim', 'axial'), may hold values from -1 to 1
- point_weight: bfloat16 [32, 32], replicated, may hold values from -1 to 1
- bias: float32 [32], replicated, may hold values from -3 to 3
Outputs:
- weight_grad: float32 [2, 16, 16, 16, 32, 32], P(None, 'azim', 'axial')
All inputs are finite; a program needn't handle non-finite values.
Results may differ from a plain program's by a relative error of at most 0.0003.
Values sent between devices are 32-bit elements; how exact they have to be, the bound alone decides.
No kernel may reach another device: no remote copies, remote signals or barrier semaphores. Data moves between devices by JAX's collectives and lax.ppermute only.
A program may use at most 128 MiB of HBM per device.

v0:
```python
import math

import jax
import jax.numpy as jnp
from jax import lax
from jax.sharding import PartitionSpec as P

NR = 64


HIGH = lax.Precision.HIGHEST


def phase_table(positions, modes, length):
    turns = positions[:, None] * modes[None, :] % length
    angle = turns.astype(jnp.float32) * (2.0 * math.pi / length)
    return (jnp.cos(angle), jnp.sin(angle))


def forward_table(cosine, sine):
    return jnp.stack([jnp.stack([cosine, -sine], 1), jnp.stack([sine, cosine], 1)], 0)


def inverse_table(cosine, sine):
    cos_t = cosine.T
    sin_t = sine.T
    return jnp.stack([jnp.stack([cos_t, sin_t], 1), jnp.stack([-sin_t, cos_t], 1)], 0)


def per_device(field, cotangent, spectral_weight, point_weight, bias):
    samples, chans, cells_a, merged = field.shape
    cells_r = NR
    cells_l = merged // cells_r
    n_azim = lax.axis_size("azim")
    n_axial = lax.axis_size("axial")
    total_a = cells_a * n_azim
    total_l = cells_l * n_axial
    loc_r = spectral_weight.shape[1]
    loc_a = spectral_weight.shape[2]
    modes = spectral_weight.shape[3]
    mode_ids = jnp.arange(modes, dtype=jnp.int32)
    cos_r, sin_r = phase_table(jnp.arange(cells_r, dtype=jnp.int32), mode_ids, cells_r)
    cos_ga, sin_ga = phase_table(jnp.arange(total_a, dtype=jnp.int32), mode_ids, total_a)
    cos_gl, sin_gl = phase_table(jnp.arange(total_l, dtype=jnp.int32), mode_ids, total_l)
    radial_fwd = jnp.stack([cos_r, -sin_r], 1)
    radial_inv = jnp.stack([cos_r.T, -sin_r.T], 0)
    forward_scale = 1.0 / math.sqrt(total_a * total_l * cells_r)
    mode_scale = 1.0 / (modes * math.sqrt(modes))

    def analysis(values):
        flat = values.reshape(samples, chans, cells_a * cells_l, cells_r)
        radial = jnp.einsum("scmz,zqr->scqrm", flat, radial_fwd, precision=HIGH)
        radial = radial.reshape(samples, chans, 2, n_azim, loc_r, cells_a * cells_l)
        radial = lax.all_to_all(radial, "azim", split_axis=3, concat_axis=5, tiled=True)
        radial = radial.reshape(samples, chans, 2, loc_r, total_a, cells_l)
        azimuth = jnp.einsum(
            "scqrxy,qxpa->scrpay", radial, forward_table(cos_ga, sin_ga), precision=HIGH
        )
        azimuth = azimuth.reshape(samples, chans, loc_r, 2, n_axial, loc_a, cells_l)
        azimuth = lax.all_to_all(azimuth, "axial", split_axis=4, concat_axis=6, tiled=True)
        azimuth = azimuth.reshape(samples, chans, loc_r, 2, loc_a, total_l)
        return jnp.einsum(
            "scrpay,pyql->scrqal", azimuth, forward_table(cos_gl, sin_gl), precision=HIGH
        )

    weight_re = spectral_weight[0].astype(jnp.float32)
    weight_im = spectral_weight[1].astype(jnp.float32)
    spectrum = analysis(field.astype(jnp.float32)) * forward_scale
    spec_re = spectrum[:, :, :, 0]
    spec_im = spectrum[:, :, :, 1]
    mixed_re = jnp.einsum("scrpl,rplco->sorpl", spec_re, weight_re, precision=HIGH) - jnp.einsum(
        "scrpl,rplco->sorpl", spec_im, weight_im, precision=HIGH
    )
    mixed_im = jnp.einsum("scrpl,rplco->sorpl", spec_re, weight_im, precision=HIGH) + jnp.einsum(
        "scrpl,rplco->sorpl", spec_im, weight_re, precision=HIGH
    )
    axial = jnp.einsum(
        "sorqal,qlpy->sorpay",
        jnp.stack([mixed_re, mixed_im], 3),
        inverse_table(cos_gl, sin_gl),
        precision=HIGH,
    )
    axial = axial.reshape(samples, chans, loc_r, 2, loc_a, n_axial, cells_l)
    axial = lax.all_to_all(axial, "axial", split_axis=5, concat_axis=4, tiled=True)
    axial = axial.reshape(samples, chans, loc_r, 2, modes, cells_l)
    cells = jnp.einsum("sorqay,qapx->sorpxy", axial, inverse_table(cos_ga, sin_ga), precision=HIGH)
    cells = cells.reshape(samples, chans, loc_r, 2, n_azim, cells_a * cells_l)
    cells = lax.all_to_all(cells, "azim", split_axis=4, concat_axis=2, tiled=True)
    cells = cells.reshape(samples, chans, modes, 2, cells_a, cells_l)
    values = jnp.einsum("sorqxy,qrz->soxyz", cells, radial_inv, precision=HIGH)
    back = values.reshape(samples, chans, cells_a, cells_l * cells_r) * mode_scale
    local_mix = jnp.einsum("oc,scxn->soxn", point_weight, field, preferred_element_type=jnp.float32)
    pre = back + local_mix + bias[None, :, None, None]
    _, pull = jax.vjp(jax.nn.gelu, pre)
    delta = pull(cotangent.astype(jnp.float32))[0]
    dmixed = analysis(delta) * mode_scale
    dmix_re = dmixed[:, :, :, 0]
    dmix_im = dmixed[:, :, :, 1]
    grad_re = jnp.einsum("scrpl,sorpl->rplco", spec_re, dmix_re, precision=HIGH) + jnp.einsum(
        "scrpl,sorpl->rplco", spec_im, dmix_im, precision=HIGH
    )
    grad_im = jnp.einsum("scrpl,sorpl->rplco", spec_re, dmix_im, precision=HIGH) - jnp.einsum(
        "scrpl,sorpl->rplco", spec_im, dmix_re, precision=HIGH
    )
    return lax.psum(jnp.stack([grad_re, grad_im]), "dp")


def solution(mesh):
    in_specs = (
        P("dp", None, "azim", "axial"),
        P("dp", None, "azim", "axial"),
        P(None, "azim", "axial", None, None, None),
        P(),
        P(),
    )
    out_specs = P(None, "azim", "axial", None, None, None)
    return jax.shard_map(
        per_device, mesh=mesh, in_specs=in_specs, out_specs=out_specs, check_vma=False
    )
```

profile of v0, /device:TPU:1, one launch (start us, length us, event | category | flops | bytes accessed | tf_op | source)
XLA Modules:
  0.0 577.3 jit_solution(7442608926419818718)
XLA Ops:
  6.6 7.1 %reshape.607 = bf16[32,512,64]{2,1,0:T(8,128)(2,1)} reshape(bf16[1,32,16,2048]{3,2,1,0:T(8,128)(2,1)} %param.5) | data formatting | bytes 4194304 | tf_op jit(solution)/shard_map/reshape
  13.7 6.4 %fusion.23 = f32[1,32,2,16,1,512]{5,3,1,2,4,0:T(8,128)S(1)} fusion(bf16[32,512,64]{2,1,0:T(8,128)(2,1)} %reshape.607, f32[64,1,16]{0,2,1:T(8,128)S(1)} %get-tuple-element.21, f32[64,1,16]{0,2,1:T(8,128)S(1)} %get-tuple-element.22), kind=kOutput, calls=%fused_computation.28 | convolution fusion | flops 402655232 | bytes 4202496 | tf_op jit(solution)/shard_map/scmz,zqr->scqrm/dot_general | solution.py:52
  20.0 2.5 copy.41
  22.6 15.8 %all-to-all-start = ((f32[1,32,2,16,1,512]{5,1,2,4,0,3:T(8,128)}), f32[1,32,2,16,1,512]{5,1,2,4,0,3:T(8,128)}, u32[]{:S(2)}, u32[]{:S(2)}) async-start(f32[1,32,2,16,1,512]{5,1,2,4,0,3:T(8,128)} %copy.41), calls=%async_computation | async-start | bytes 4194304 | tf_op jit(solution)/shard_map/all_to_all | solution.py:54
  39.0 91.3 %all-to-all-done = f32[1,32,2,16,1,512]{5,1,2,4,0,3:T(8,128)} async-done(((f32[1,32,2,16,1,512]{5,1,2,4,0,3:T(8,128)}), f32[1,32,2,16,1,512]{5,1,2,4,0,3:T(8,128)}, u32[]{:S(2)}, u32[]{:S(2)}) %all-to-all-start) | async-done | bytes 2097184 | tf_op jit(solution)/shard_map/all_to_all | solution.py:54
  130.3 2.8 copy.42
  133.1 4.4 reshape.609
  137.5 7.2 %fusion.6 = f32[2,16,32,32,1]{3,1,4,2,0:T(8,128)S(1)} fusion(f32[32,2,256,32]{3,2,1,0:T(8,128)} %reshape.609, f32[1,256,2,16]{1,3,0,2:T(8,128)S(1)} %get-tuple-element.16, f32[1,256,2,16]{1,3,0,2:T(8,128)S(1)} %get-tuple-element.15), kind=kOutput, calls=%fused_computation.7 | convolution fusion | flops 201342976 | bytes 2293760 | tf_op jit(solution)/shard_map/scqrxy,qxpa->scrpay/dot_general | solution.py:56
  145.8 4.4 all-to-all-start.1
  150.3 4.7 all-to-all-done.1
  161.7 3.3 all-to-all-start.2
  165.0 4.8 all-to-all-done.2
  171.4 1.8 convolution_bitcast_fusion
  173.2 4.7 copy.51
  177.9 6.2 %reshape.619 = f32[1,32,1,2,16,512]{5,4,3,1,2,0:T(8,128)S(1)} reshape(f32[1,32,1,2,256,32]{5,4,3,1,2,0:T(8,128)} %copy.51) | data formatting | bytes 4194304 | tf_op jit(solution)/shard_map/reshape | solution.py:87
  184.1 2.9 copy.52
  187.1 11.1 %all-to-all-start.3 = ((f32[1,32,1,2,16,512]{5,3,1,2,0,4:T(2,128)}), f32[1,32,1,2,16,512]{5,3,1,2,0,4:T(2,128)S(1)}, u32[]{:S(2)}, u32[]{:S(2)}) async-start(f32[1,32,1,2,16,512]{5,3,1,2,0,4:T(2,128)} %copy.52), calls=%async_computation.3 | async-start | bytes 4194304 | tf_op jit(solution)/shard_map/all_to_all | solution.py:88
  198.6 91.5 %all-to-all-done.3 = f32[1,32,1,2,16,512]{5,3,1,2,0,4:T(2,128)S(1)} async-done(((f32[1,32,1,2,16,512]{5,3,1,2,0,4:T(2,128)}), f32[1,32,1,2,16,512]{5,3,1,2,0,4:T(2,128)S(1)}, u32[]{:S(2)}, u32[]{:S(2)}) %all-to-all-start.3) | async-done | bytes 2097184 | tf_op jit(solution)/shard_map/all_to_all | solution.py:88
  290.1 5.2 reshape.658
  295.2 21.1 %bitcast_multiply_fusion = f32[32,16,32,64]{3,2,1,0:T(8,128)} fusion(f32[32,16,2,16,32]{4,3,2,0,1:T(8,128)} %reshape.658, f32[1,16,64]{2,1,0:T(8,128)S(1)} %get-tuple-element.31, f32[1,16,64]{2,1,0:T(8,128)S(1)} %get-tuple-element.32), kind=kOutput, calls=%fused_computation.4 | convolution fusion | flops 403703808 | bytes 6299648 | tf_op jit(solution)/shard_map/sorqxy,qrz->soxyz/dot_general | solution.py:90
  316.4 8.0 %mul.493 = f32[1,32,16,2048]{3,2,1,0:T(8,128)} reshape(f32[32,16,32,64]{3,2,1,0:T(8,128)} %bitcast_multiply_fusion) | data formatting | bytes 8388608 | tf_op jit(solution)/shard_map/mul | solution.py:91
  324.4 11.4 %fusion.9 = f32[1,32,16,2048]{3,1,2,0:T(8,128)S(1)} fusion(f32[1,32,16,2048]{3,2,1,0:T(8,128)} %mul.493, bf16[32,16,2048]{2,1,0:T(8,128)(2,1)S(1)} %bitcast.284, bf16[1,32,16,2048]{3,2,1,0:T(8,128)(2,1)} %param.6, f32[32]{0:T(128)S(1)} %copy-done.4, bf16[32,32]{1,0:T(8,128)(2,1)S(1)} %copy-done), kind=kOutput, calls=%fused_computation.14 | convolution fusion | flops 90177536 | bytes 12585088 | tf_op jit(solution)/shard_map/oc,scxn->soxn/dot_general | solution.py:92
  335.8 4.4 copy.57
  340.2 7.9 %reshape.622 = f32[32,512,64]{2,1,0:T(8,128)} reshape(f32[1,32,16,2048]{3,2,1,0:T(8,128)} %copy.57) | data formatting | bytes 8388608 | tf_op jit(solution)/shard_map/reshape.49
  348.0 10.8 %fusion.26 = f32[1,32,2,16,1,512]{5,3,1,2,4,0:T(8,128)S(1)} fusion(f32[32,512,64]{2,1,0:T(8,128)} %reshape.622, f32[64,1,16]{0,2,1:T(8,128)S(1)} %get-tuple-element.21, f32[64,1,16]{0,2,1:T(8,128)S(1)} %get-tuple-element.22), kind=kOutput, calls=%fused_computation.29 | convolution fusion | flops 402655232 | bytes 6299648 | tf_op jit(solution)/shard_map/scmz,zqr->scqrm/dot_general | solution.py:52
  360.1 101.3 %all_to_all.78 = f32[1,32,2,16,1,512]{5,1,2,4,0,3:T(8,128)S(1)} all-to-all(f32[1,32,2,16,1,512]{5,1,2,4,0,3:T(8,128)S(1)} %copy.59), channel_id=1, replica_groups=mesh['dp'=8,'azim'=16,'axial'=4] {'azim'}, dimensions={3} | all-to-all | bytes 4194304 | tf_op jit(solution)/shard_map/all_to_all | solution.py:54
  462.6 4.4 reshape.624
  467.1 7.2 %fusion = f32[2,16,32,32,1]{3,1,4,2,0:T(8,128)S(1)} fusion(f32[32,2,256,32]{3,2,1,0:T(8,128)} %reshape.624, f32[1,256,2,16]{1,3,0,2:T(8,128)S(1)} %get-tuple-element.16, f32[1,256,2,16]{1,3,0,2:T(8,128)S(1)} %get-tuple-element.15), kind=kOutput, calls=%fused_computation | convolution fusion | flops 201342976 | bytes 2293760 | tf_op jit(solution)/shard_map/scqrxy,qxpa->scrpay/dot_general | solution.py:56
  474.7 7.2 %all_to_all.79 = f32[4,1,8192]{2,1,0:T(1,128)S(1)} all-to-all(f32[4,1,8192]{2,1,0:T(1,128)S(1)} %reshape.664), channel_id=1, replica_groups=mesh['dp'=8,'azim'=16,'axial'=4] {'axial'}, dimensions={0} | all-to-all | bytes 262144 | tf_op jit(solution)/shard_map/all_to_all | solution.py:60
  484.9 1.6 pad_maximum_fusion
  486.5 80.7 %all-reduce.2.cloned.1.call-done = f32[2,1,4,16,32,32]{5,4,3,2,1,0:T(8,128)} async-done(((f32[2,1,4,16,32,32]{5,4,3,2,1,0:T(8,128)}), f32[2,1,4,16,32,32]{5,4,3,2,1,0:T(8,128)}) %all-reduce.2.cloned.1.call-update) | async-done | bytes 524304 | tf_op jit(solution)/shard_map/psum | solution.py:105
  567.2 3.1 copy.110
  (62 shorter events, 16.1 us)
Async XLA Ops:
  6.5 317.8 %copy-start = (bf16[32,32]{1,0:T(8,128)(2,1)S(1)}, bf16[32,32]{1,0:T(8,128)(2,1)}, u32[]{:S(2)}) copy-start(bf16[32,32]{1,0:T(8,128)(2,1)} %param.8) | copy-start | bytes 6148
  22.6 107.7 %all-to-all-start = ((f32[1,32,2,16,1,512]{5,1,2,4,0,3:T(8,128)}), f32[1,32,2,16,1,512]{5,1,2,4,0,3:T(8,128)}, u32[]{:S(2)}, u32[]{:S(2)}) async-start(f32[1,32,2,16,1,512]{5,1,2,4,0,3:T(8,128)} %copy.41), calls=%async_computation | async-start | bytes 4194304 | tf_op jit(solution)/shard_map/all_to_all | solution.py:54
  144.7 13.3 %copy-start.3 = (bf16[2,1,4,16,32,32]{5,4,3,2,1,0:T(8,128)(2,1)S(1)}, bf16[2,1,4,16,32,32]{5,4,3,2,1,0:T(8,128)(2,1)}, u32[]{:S(2)}) copy-start(bf16[2,1,4,16,32,32]{5,4,3,2,1,0:T(8,128)(2,1)} %param.7) | copy-start | bytes 786436
  145.8 9.2 %all-to-all-start.1 = ((f32[4,1,8192]{2,1,0:T(1,128)}), f32[4,1,8192]{2,1,0:T(1,128)S(1)}, u32[]{:S(2)}, u32[]{:S(2)}) async-start(f32[4,1,8192]{2,1,0:T(1,128)} %reshape.660), calls=%async_computation.1 | async-start | bytes 262144 | tf_op jit(solution)/shard_map/all_to_all | solution.py:60
  161.7 8.1 %all-to-all-start.2 = ((f32[4,1,8192]{2,1,0:T(1,128)}), f32[4,1,8192]{2,1,0:T(1,128)S(1)}, u32[]{:S(2)}, u32[]{:S(2)}) async-start(f32[4,1,8192]{2,1,0:T(1,128)} %reshape.662), calls=%async_computation.2 | async-start | bytes 262144 | tf_op jit(solution)/shard_map/all_to_all | solution.py:84
  187.1 103.0 %all-to-all-start.3 = ((f32[1,32,1,2,16,512]{5,3,1,2,0,4:T(2,128)}), f32[1,32,1,2,16,512]{5,3,1,2,0,4:T(2,128)S(1)}, u32[]{:S(2)}, u32[]{:S(2)}) async-start(f32[1,32,1,2,16,512]{5,3,1,2,0,4:T(2,128)} %copy.52), calls=%async_computation.3 | async-start | bytes 4194304 | tf_op jit(solution)/shard_map/all_to_all | solution.py:88
  198.2 369.0 %all-reduce.2.cloned.1.call-start = ((), (), s32[]{:S(2)}) async-start(), calls=%async_computation.6 | async-start | bytes 4194304 | tf_op jit(solution)/shard_map/psum | solution.py:105
  316.4 8.0 %copy-start.2 = (bf16[1,32,16,2048]{3,2,1,0:T(8,128)(2,1)S(1)}, bf16[1,32,16,2048]{3,2,1,0:T(8,128)(2,1)}, u32[]{:S(2)}) copy-start(bf16[1,32,16,2048]{3,2,1,0:T(8,128)(2,1)} %param.5) | copy-start | bytes 6291460
  316.4 8.0 %copy-start.4 = (f32[32]{0:T(128)S(1)}, f32[32]{0:T(128)}, u32[]{:S(2)}) copy-start(f32[32]{0:T(128)} %param.9) | copy-start | bytes 388
  484.9 85.4 %copy-start.1 = (bf16[32,32]{1,0:T(8,128)(2,1)S(1)}, bf16[32,32]{1,0:T(8,128)(2,1)}, u32[]{:S(2)}) copy-start(bf16[32,32]{1,0:T(8,128)(2,1)} %param.8) | copy-start | bytes 6148
Sparse Core Ops, SparseCore 0:
  486.7 80.4 all-reduce.1
where the time goes:
time: 586 us; the launch traced here: 577 us
  waiting for transfers between devices  273 us (47%)
  blocking collectives  109 us (19%)
  local copies, waits for them, and re-layouts  71.8 us (12%)
  matrix products  69.1 us (12%)
  starting transfers between devices  34.9 us (6%)
  between operations  14 us (2%)
  other arithmetic  5.97 us (1%)
    all_to_all x1, blocking collectives, analysis(): lax.all_to_all(radial, 'azim', split_axis=3, concat_axis=5, tiled=True)  101 us
    all_to_all x1, waiting for transfers between devices, per_device(): lax.all_to_all(cells, 'azim', split_axis=4, concat_axis=2, tiled=True)  91.5 us
    all_to_all x1, waiting for transfers between devices, analysis(): lax.all_to_all(radial, 'azim', split_axis=3, concat_axis=5, tiled=True)  91.3 us
    psum x1, waiting for transfers between devices, per_device(): return lax.psum(jnp.stack([grad_re, grad_im]), 'dp')  80.7 us
    another operation x8, local copies, waits for them, and re-layouts  22.4 us
    dot_general x1, matrix products, per_device(): values = jnp.einsum('sorqxy,qrz->soxyz', cells, radial_inv, precision=HIGH)  21.1 us
    dot_general x2, matrix products, analysis(): radial = jnp.einsum('scmz,zqr->scqrm', flat, radial_fwd, precision=HIGH)  17.2 us
    all_to_all x1, starting transfers between devices, analysis(): lax.all_to_all(radial, 'azim', split_axis=3, concat_axis=5, tiled=True)  15.8 us
  transfers between devices with their start and end apart: 5, of which 5 were waited for; matrix products, arithmetic and copies ran while one was open for 0% of the time, Pallas kernels for 0%

commit v1 on v0

v1 whole, which is shorter than its diff:
```python
import math

import jax
import jax.numpy as jnp
import ml_dtypes
import numpy as np
from jax import lax
from jax.experimental import pallas as pl
from jax.experimental.pallas import tpu as pltpu
from jax.sharding import PartitionSpec as P

NR = 64
BF = jnp.bfloat16
F32 = jnp.float32
LANE_STEPS = 4
VMEM = 60 * 1024 * 1024


def split_table(values):
    high = values.astype(ml_dtypes.bfloat16)
    low = (values - high.astype(np.float64)).astype(ml_dtypes.bfloat16)
    return high, low


def split(values):
    high = values.astype(BF)
    return high, (values - high.astype(F32)).astype(BF)


def split3(values):
    high = values.astype(BF)
    rest = values - high.astype(F32)
    mid = rest.astype(BF)
    return high, mid, (rest - mid.astype(F32)).astype(BF)


def dot(a, b):
    return lax.dot_general(a, b, (((1,), (0,)), ((), ())), preferred_element_type=F32)


def dot_nt(a, b):
    return lax.dot_general(a, b, (((1,), (1,)), ((), ())), preferred_element_type=F32)


def dot_tn(a, b):
    return lax.dot_general(a, b, (((0,), (0,)), ((), ())), preferred_element_type=F32)


class Tables:
    def __init__(self, modes, chans, cells_a, cells_l, cells_r, n_azim, n_axial):
        total_a, total_l = cells_a * n_azim, cells_l * n_axial
        k = np.arange(modes, dtype=np.float64)
        radial = np.outer(k, np.arange(cells_r)) / cells_r
        axial = np.outer(k, np.arange(cells_l)) / total_l
        angle = 2.0 * np.pi * (radial[:, None, None, :] + axial[None, :, :, None])
        angle = angle.reshape(modes * modes, cells_l * cells_r)
        self.cells = split_table(np.concatenate([np.cos(angle), -np.sin(angle)], 0))
        angle = 2.0 * np.pi * np.outer(np.arange(cells_a), k) / total_a
        same = np.eye(chans)

        def spread(table):
            whole = table[None, :, :, None] * same[:, None, None, :]
            return whole.reshape(chans * cells_a, modes * chans)

        self.turn = split_table(spread(np.cos(angle))) + split_table(spread(np.sin(angle)))
        quarter = 0.5 * np.pi * (np.outer(np.arange(n_axial), k) % 4 if n_axial == 4 else np.outer(np.arange(n_axial), k) * (4 / n_axial))
        self.axial_cos = np.repeat(np.cos(quarter).round(15)[:, :, None], 128, 2).astype(np.float32)
        self.axial_sin = np.repeat(np.sin(quarter).round(15)[:, :, None], 128, 2).astype(np.float32)
        loc_a = modes // n_axial
        turns = np.outer(np.arange(n_azim), k) / n_azim
        turns = turns.reshape(n_azim, n_axial, loc_a).transpose(1, 0, 2)
        turns = np.repeat(turns, chans, 2) * (2.0 * np.pi)
        self.azim_cos = np.cos(turns).astype(np.float32)
        self.azim_sin = np.sin(turns).astype(np.float32)


def azimuth_analysis(values, turn, out_ref):
    cos_h, cos_l, sin_h, sin_l = (r[...] for r in turn)
    high, low = split(values)
    by_cos = dot(high, cos_h) + dot(low, cos_h) + dot(high, cos_l)
    by_sin = dot(high, sin_h) + dot(low, sin_h) + dot(high, sin_l)
    half = values.shape[0] // 2
    real = by_cos[:half] + by_sin[half:]
    imag = by_cos[half:] - by_sin[:half]
    groups, n_kr, rows, lanes = out_ref.shape
    n_kl = rows // 2
    for g in range(groups):
        at = slice(g * lanes, (g + 1) * lanes)
        out_ref[g, :, :n_kl, :] = real[:, at].reshape(n_kr, n_kl, lanes)
        out_ref[g, :, n_kl:, :] = imag[:, at].reshape(n_kr, n_kl, lanes)


def analysis_kernel(field, cells_h, cells_l, cos_h, cos_l, sin_h, sin_l, out, total):
    step = pl.program_id(0)
    x = field[...]
    part = dot_nt(cells_h[...], x) + dot_nt(cells_l[...], x)

    @pl.when(step == 0)
    def _():
        total[...] = part

    @pl.when(step > 0)
    def _():
        total[...] += part

    @pl.when(step == pl.num_programs(0) - 1)
    def _():
        azimuth_analysis(total[...], (cos_h, cos_l, sin_h, sin_l), out)


def layer_kernel(
    mixed, field, cot, mix, bias, cells_h, cells_l, cos_h, cos_l, sin_h, sin_l, out, synth_h, synth_l, total
):
    step = pl.program_id(0)

    @pl.when(step == 0)
    def _():
        groups, n_kr, rows, lanes = mixed.shape
        n_kl = rows // 2

        def gather(at):
            parts = [mixed[g, :, at, :].reshape(n_kr * n_kl, lanes) for g in range(groups)]
            return jnp.concatenate(parts, 1)

        re_h, re_l = split(gather(slice(0, n_kl)))
        im_h, im_l = split(gather(slice(n_kl, rows)))
        c_h, c_l, s_h, s_l = cos_h[...], cos_l[...], sin_h[...], sin_l[...]

        def times(t_h, t_l, v_h, v_l):
            return dot_nt(t_h, v_h) + dot_nt(t_h, v_l) + dot_nt(t_l, v_h)

        real = times(c_h, c_l, re_h, re_l) - times(s_h, s_l, im_h, im_l)
        imag = times(s_h, s_l, re_h, re_l) + times(c_h, c_l, im_h, im_l)
        half = real.shape[1]
        high, low = split(real)
        synth_h[:, :half] = high
        synth_l[:, :half] = low
        high, low = split(imag)
        synth_h[:, half:] = high
        synth_l[:, half:] = low

    t_h = cells_h[...]
    t_l = cells_l[...]
    s_h = synth_h[...]
    pre = dot(s_h, t_h) + dot(synth_l[...], t_h) + dot(s_h, t_l)
    pre = pre + dot(mix[...], field[...]) + bias[...]
    slope = math.sqrt(2.0 / math.pi)
    square = pre * pre
    t = jnp.tanh(pre * (slope + (slope * 0.044715) * square))
    inner = slope + (3.0 * slope * 0.044715) * square
    grad = 0.5 * (1.0 + t) + (0.5 * pre) * (1.0 - t * t) * inner
    d_h, d_l = split(cot[...].astype(F32) * grad)
    part = dot_nt(t_h, d_h) + dot_nt(t_h, d_l) + dot_nt(t_l, d_h)

    @pl.when(step == 0)
    def _():
        total[...] = part

    @pl.when(step > 0)
    def _():
        total[...] += part

    @pl.when(step == pl.num_programs(0) - 1)
    def _():
        azimuth_analysis(total[...], (cos_h, cos_l, sin_h, sin_l), out)


def axial_sum_kernel(parts, cos, sin, out):
    groups, _, rows, _ = parts.shape
    n_kl = rows // 2
    real = parts[0, :, :n_kl, :]
    imag = parts[0, :, n_kl:, :]
    for g in range(1, groups):
        re, im = parts[g, :, :n_kl, :], parts[g, :, n_kl:, :]
        c, s = cos[g][None], sin[g][None]
        real += re * c + im * s
        imag += im * c - re * s
    out[:, :n_kl, :] = real
    out[:, n_kl:, :] = imag


def axial_spread_kernel(values, cos, sin, out):
    groups, _, rows, _ = out.shape
    n_kl = rows // 2
    re, im = values[:, :n_kl, :], values[:, n_kl:, :]
    for g in range(groups):
        c, s = cos[g][None], sin[g][None]
        out[g, :, :n_kl, :] = re * c - im * s
        out[g, :, n_kl:, :] = im * c + re * s


def azim_sum(parts, cos, sin, n_kl, scale):
    real = imag = None
    for z in range(parts.shape[0]):
        re, im = parts[z, :n_kl, :], parts[z, n_kl:, :]
        c, s = cos[z : z + 1, :], sin[z : z + 1, :]
        a, b = re * c + im * s, im * c - re * s
        real, imag = (a, b) if z == 0 else (real + a, imag + b)
    return real * scale, imag * scale


def mix_kernel(scale, out_scale, parts, weight, cos, sin, spec, out):
    n_azim, rows, lanes = parts.shape
    n_kl = rows // 2
    y = lax.axis_index("axial")
    c, s = cos[y], sin[y]
    real, imag = azim_sum(parts, c, s, n_kl, scale)
    spec[:n_kl, :] = real
    spec[n_kl:, :] = imag
    stack = jnp.concatenate([*split3(real), *split3(imag)], 0)
    row = lax.broadcasted_iota(jnp.int32, (stack.shape[0], 2 * lanes), 0) % n_kl
    got = jnp.zeros((stack.shape[0], 2 * lanes), F32)
    for kl in range(n_kl):
        got = jnp.where(row == kl, dot(stack, weight[kl]), got)
    by_re = got[:n_kl] + got[n_kl : 2 * n_kl] + got[2 * n_kl : 3 * n_kl]
    by_im = got[3 * n_kl : 4 * n_kl] + got[4 * n_kl : 5 * n_kl] + got[5 * n_kl :]
    re = (by_re[:, :lanes] - by_im[:, lanes:]) * out_scale
    im = (by_re[:, lanes:] + by_im[:, :lanes]) * out_scale
    for z in range(n_azim):
        cz, sz = c[z : z + 1, :], s[z : z + 1, :]
        out[z, :n_kl, :] = re * cz - im * sz
        out[z, n_kl:, :] = im * cz + re * sz


def join_kernel(scale, parts, spec, cos, sin, out):
    rows = parts.shape[1]
    n_kl = rows // 2
    y = lax.axis_index("axial")
    real, imag = azim_sum(parts, cos[y], sin[y], n_kl, scale)
    for d in range(out.shape[0]):
        out[d, :rows, :] = spec[...]
        out[d, rows : rows + n_kl, :] = real
        out[d, rows + n_kl :, :] = imag


def grad_kernel(pairs, out):
    _, n_ka, n_kl, chans, _ = out.shape
    lanes = pairs.shape[2]
    for kl in range(n_kl):
        s_re, s_im, d_re, d_im = (pairs[:, i * n_kl + kl, :] for i in range(4))
        s_h, s_l = split(jnp.concatenate([s_re, s_im], 0))
        a = jnp.concatenate([d_re, d_im], 0)
        b = jnp.concatenate([d_im, -d_re], 0)
        d_h, d_l = split(jnp.concatenate([a, b], 1))
        left = jnp.concatenate([s_h, s_l, s_h], 0)
        right = jnp.concatenate([d_h, d_h, d_l], 0)
        whole = dot_tn(left, right)
        for ka in range(n_ka):
            at = slice(ka * chans, (ka + 1) * chans)
            for q in range(2):
                lo = q * lanes + ka * chans
                out[q, ka, kl] = whole[at, lo : lo + chans]


def call(kernel, out_shape, *args, **more):
    return pl.pallas_call(
        kernel,
        out_shape=out_shape,
        compiler_params=pltpu.CompilerParams(vmem_limit_bytes=VMEM),
        **more,
    )(*args)


def per_device(field, cotangent, spectral_weight, point_weight, bias):
    samples, chans, cells_a, merged = field.shape
    cells_r = NR
    cells_l = merged // cells_r
    n_azim = lax.axis_size("azim")
    n_axial = lax.axis_size("axial")
    n_dp = lax.axis_size("dp")
    _, _, loc_a, modes, _, _ = spectral_weight.shape
    tables = Tables(modes, chans, cells_a, cells_l, cells_r, n_azim, n_axial)
    total_cells = cells_a * n_azim * cells_l * n_axial * cells_r
    forward_scale = 1.0 / math.sqrt(total_cells)
    mode_scale = 1.0 / (modes * math.sqrt(modes))
    rows_x = chans * cells_a
    rows_k = 2 * modes * modes
    lanes = loc_a * chans
    block = (2 * modes, lanes)
    whole = jax.ShapeDtypeStruct((n_axial, modes, *block), F32)
    ring = jax.ShapeDtypeStruct((n_azim, *block), F32)
    cells = [jnp.asarray(t) for t in tables.cells]
    turn = [jnp.asarray(t) for t in tables.turn]
    axial_phase = (jnp.asarray(tables.axial_cos), jnp.asarray(tables.axial_sin))
    azim_phase = (jnp.asarray(tables.azim_cos), jnp.asarray(tables.azim_sin))

    x = field.reshape(rows_x, merged)
    cot = cotangent.reshape(rows_x, merged)
    weight = spectral_weight[:, 0].transpose(2, 1, 3, 0, 4)
    weight = weight[:, :, :, :, None, :] * jnp.eye(loc_a, dtype=BF)[None, :, None, None, :, None]
    weight = weight.reshape(modes, lanes, 2 * lanes)
    mix = point_weight[:, None, :, None] * jnp.eye(cells_a, dtype=BF)[None, :, None, :]
    mix = mix.reshape(rows_x, rows_x)
    bias_rows = jnp.repeat(bias, cells_a)[:, None]

    step = merged // LANE_STEPS
    lane_spec = pl.BlockSpec((rows_x, step), lambda i: (0, i))
    cell_spec = pl.BlockSpec((rows_k, step), lambda i: (0, i))

    def fixed(array):
        return pl.BlockSpec(array.shape, lambda i: (0,) * array.ndim)

    total = pltpu.VMEM((rows_k, rows_x), F32)

    def reduce(values):
        values = lax.all_to_all(values, "axial", 0, 0, tiled=True)
        values = call(axial_sum_kernel, ring, values, *axial_phase)
        return lax.all_to_all(values, "azim", 0, 0, tiled=True)

    first = call(
        analysis_kernel,
        whole,
        x,
        *cells,
        *turn,
        grid=(LANE_STEPS,),
        in_specs=[lane_spec, cell_spec, cell_spec, *map(fixed, turn)],
        out_specs=fixed(whole),
        scratch_shapes=[total],
    )
    parts = reduce(first)

    def mix_body(*refs):
        mix_kernel(forward_scale, mode_scale, *refs)

    spec, mixed = call(
        mix_body, (jax.ShapeDtypeStruct(block, F32), ring), parts, weight, *azim_phase
    )
    mixed = lax.all_to_all(mixed, "azim", 0, 0, tiled=True)
    mixed = call(axial_spread_kernel, whole, mixed, *axial_phase)
    mixed = lax.all_to_all(mixed, "axial", 0, 0, tiled=True)
    synth = pltpu.VMEM((rows_x, rows_k), BF)
    second = call(
        layer_kernel,
        whole,
        mixed,
        x,
        cot,
        mix,
        bias_rows,
        *cells,
        *turn,
        grid=(LANE_STEPS,),
        in_specs=[fixed(whole), lane_spec, lane_spec, fixed(mix), fixed(bias_rows), cell_spec, cell_spec, *map(fixed, turn)],
        out_specs=fixed(whole),
        scratch_shapes=[synth, synth, total],
    )
    parts = reduce(second)

    def join_body(*refs):
        join_kernel(mode_scale, *refs)

    pairs = call(
        join_body, jax.ShapeDtypeStruct((n_dp, 2 * block[0], lanes), F32), parts, spec, *azim_phase
    )
    pairs = lax.all_to_all(pairs, "dp", 0, 0, tiled=True)
    grad = call(grad_kernel, jax.ShapeDtypeStruct((2, loc_a, modes, chans, chans), F32), pairs)
    return grad[:, None]


def solution(mesh):
    in_specs = (
        P("dp", None, "azim", "axial"),
        P("dp", None, "azim", "axial"),
        P(None, "azim", "axial", None, None, None),
        P(),
        P(),
    )
    out_specs = P(None, "azim", "axial", None, None, None)
    return jax.shard_map(
        per_device, mesh=mesh, in_specs=in_specs, out_specs=out_specs, check_vma=False
    )
```

time: 586 us -> 189 us (0.32); the launches traced: 577 us -> 188 us
  waiting for transfers between devices: 273 us -> 0.35 us
  matrix products: 69.1 us -> 0 us
  local copies, waits for them, and re-layouts: 71.8 us -> 22.4 us
  Pallas kernels: 0 us -> 41.3 us
  between operations: 14 us -> 0.1 us
  blocking collectives: 109 us -> 97.2 us
  starting transfers between devices: 34.9 us -> 23.1 us
    all_to_all x4 -> x2, waiting for transfers between devices: 192 us -> 0.35 us  [the longest x1 0.34 us: reduce(): return lax.all_to_all(values, 'azim', 0, 0, tiled=True)]
    psum x1 -> x0, waiting for transfers between devices: 80.7 us -> none  [per_device(): return lax.psum(jnp.stack([grad_re, grad_im]), 'dp')]
    dot_general x14 -> x0, matrix products: 69.1 us -> none  [the longest x1 21.1 us: per_device(): values = jnp.einsum('sorqxy,qrz->soxyz', cells, radial_inv, precision=HIGH)]
    pallas_call x0 -> x8, Pallas kernels: none -> 41.3 us  [call(): pl.pallas_call(kernel, out_shape=out_shape, compiler_params=pltpu.Compile...]
    another operation x8 -> x1, local copies, waits for them, and re-layouts: 22.4 us -> 0.88 us  [per_device(): bias_rows = jnp.repeat(bias, cells_a)[:, None]]
    reshape x9 -> x0, local copies, waits for them, and re-layouts: 20.5 us -> none  [the longest x2 9.18 us: per_device(): cells = cells.reshape(samples, chans, loc_r, 2, n_azim, cells_a * cells_l)]
    all_to_all x4 -> x2, starting transfers between devices: 34.6 us -> 23.1 us  [the longest x1 19.4 us: reduce(): return lax.all_to_all(values, 'azim', 0, 0, tiled=True)]
    all_to_all x2 -> x5, blocking collectives: 109 us -> 97.2 us  [the longest x2 29 us: reduce(): values = lax.all_to_all(values, 'axial', 0, 0, tiled=True)]
  transfers between devices with their start and end apart: 5 -> 2, of which waited for: 5 -> 1; matrix products, arithmetic and copies ran while one was open for 0% -> 13% of each run, Pallas kernels for 0% -> 0%
where the time goes in v1:
time: 189 us; the launch traced here: 188 us
  blocking collectives  97.2 us (51%)
  Pallas kernels  41.3 us (22%)
  starting transfers between devices  23.1 us (12%)
  local copies, waits for them, and re-layouts  22.4 us (12%)
  other arithmetic  3.35 us (2%)
    pallas_call x8, Pallas kernels, call(): pl.pallas_call(kernel, out_shape=out_shape, compiler_params=pltpu.Compile...  41.3 us
    all_to_all x2, blocking collectives, reduce(): values = lax.all_to_all(values, 'axial', 0, 0, tiled=True)  29 us
    all_to_all x1, blocking collectives, reduce(): return lax.all_to_all(values, 'azim', 0, 0, tiled=True)  26.4 us
    all_to_all x1, blocking collectives, per_device(): mixed = lax.all_to_all(mixed, 'azim', 0, 0, tiled=True)  24 us
    all_to_all x1, starting transfers between devices, reduce(): return lax.all_to_all(values, 'azim', 0, 0, tiled=True)  19.4 us
    all_to_all x1, blocking collectives, per_device(): pairs = lax.all_to_all(pairs, 'dp', 0, 0, tiled=True)  17.8 us
    mul x4, local copies, waits for them, and re-layouts, per_device(): weight[:, :, :, :, None, :]  10.3 us
    mul x1, local copies, waits for them, and re-layouts, per_device(): point_weight[:, None, :, None]  8.4 us
  transfers between devices with their start and end apart: 2, of which 1 were waited for; matrix products, arithmetic and copies ran while one was open for 13% of the time, Pallas kernels for 0%

profile of v1, /device:TPU:1, one launch (start us, length us, event | category | flops | bytes accessed | tf_op | source)
XLA Modules:
  0.0 187.7 jit_solution(5822061433682079041)
XLA Ops:
  0.0 9.1 %shard_map.145 = f32[4,16,32,128]{3,2,1,0:T(8,128)} custom-call(bf16[512,2048]{1,0:T(8,128)(2,1)} %bitcast.10, bf16[512,2048]{1,0:T(8,128)(2,1)} %constant.20.clone.cells_h, bf16[512,2048]{1,0:T(8,128)(2,1)} %constant.21.clone.cells_l, bf16[512,512]{1,0:T(8,128)(2,1)} %constant.22.clone.cos_h, bf16[512,512]{1,0:T(8,128)(2,1)} %constant.23.clone.cos_l, ...), custom_call_target="tpu_custom_call" | custom-call | tf_op jit(solution)/shard_map/pallas_call | solution.py:256
  9.1 15.0 %all_to_all.35.parts = f32[4,16,32,128]{3,2,1,0:T(8,128)} all-to-all(f32[4,16,32,128]{3,2,1,0:T(8,128)} %shard_map.145), channel_id=1, replica_groups=mesh['dp'=8,'azim'=16,'axial'=4] {'axial'}, dimensions={0} | all-to-all | bytes 2097152 | tf_op jit(solution)/shard_map/all_to_all | solution.py:306
  24.0 2.1 %shard_map.146 = f32[16,32,128]{2,1,0:T(8,128)} custom-call(f32[4,16,32,128]{3,2,1,0:T(8,128)} %all_to_all.35.parts, f32[4,16,128]{2,1,0:T(8,128)} %constant.26.clone.cos, f32[4,16,128]{2,1,0:T(8,128)} %constant.27.clone.sin), custom_call_target="tpu_custom_call" | custom-call | tf_op jit(solution)/shard_map/pallas_call | solution.py:256
  26.1 19.4 %all-to-all-start.1 = ((f32[16,32,128]{2,1,0:T(8,128)}), f32[16,32,128]{2,1,0:T(8,128)S(1)}, u32[]{:S(2)}, u32[]{:S(2)}) async-start(f32[16,32,128]{2,1,0:T(8,128)} %shard_map.146), calls=%async_computation.1 | async-start | bytes 524288 | tf_op jit(solution)/shard_map/all_to_all | solution.py:308
  45.5 0.0 copy-done.1
  45.5 1.1 copy.18
  46.6 3.7 %mul.37 = bf16[16,4,32,2,4,32]{5,4,3,2,1,0:T(4,128)(2,1)} broadcast(bf16[16,4,32,2,32]{4,3,2,1,0:T(2,128)(2,1)S(1)} %copy.18), dimensions={0,1,2,3,5} | broadcast | bytes 1310720 | tf_op jit(solution)/shard_map/mul | solution.py:290
  50.3 6.2 %mul.38 = bf16[16,128,256]{2,1,0:T(8,128)(2,1)S(1)} reshape(bf16[16,4,32,2,4,32]{5,4,3,2,1,0:T(4,128)(2,1)} %mul.37) | data formatting | bytes 2097152 | tf_op jit(solution)/shard_map/mul | solution.py:290
  56.5 0.0 copy-start.3
  56.6 0.1 mul.39
  56.7 0.2 mul.40
  56.9 1.0 broadcast_multiply_fusion.1.refs_1_
  57.9 0.3 all-to-all-done.1.refs_0_
  58.3 0.7 copy-done.2
  59.0 2.4 %shard_map.147 = (f32[32,128]{1,0:T(8,128)}, f32[16,32,128]{2,1,0:T(8,128)}) custom-call(f32[16,32,128]{2,1,0:T(8,128)} %copy-done.2, bf16[16,128,256]{2,1,0:T(8,128)(2,1)} %broadcast_multiply_fusion.1.refs_1_, f32[4,16,128]{2,1,0:T(8,128)} %constant.28.clone.refs_2_, f32[4,16,128]{2,1,0:T(8,128)} %constant.29.clone.refs_3_), custom_call_target="tpu_custom_call" | custom-call | tf_op jit(solution)/shard_map/pallas_call | solution.py:256
  61.4 24.0 %all_to_all.36.values = f32[16,32,128]{2,1,0:T(8,128)} all-to-all(f32[16,32,128]{2,1,0:T(8,128)} %get-tuple-element.7), channel_id=1, replica_groups=mesh['dp'=8,'azim'=16,'axial'=4] {'azim'}, dimensions={0} | all-to-all | bytes 524288 | tf_op jit(solution)/shard_map/all_to_all | solution.py:329
  85.4 2.1 %shard_map.148 = f32[4,16,32,128]{3,2,1,0:T(8,128)} custom-call(f32[16,32,128]{2,1,0:T(8,128)} %all_to_all.36.values, f32[4,16,128]{2,1,0:T(8,128)} %constant.26.clone.cos, f32[4,16,128]{2,1,0:T(8,128)} %constant.27.clone.sin), custom_call_target="tpu_custom_call" | custom-call | tf_op jit(solution)/shard_map/pallas_call | solution.py:256
  87.4 3.7 %all-to-all-start.3 = ((f32[4,16,32,128]{3,2,1,0:T(8,128)}), f32[4,16,32,128]{3,2,1,0:T(8,128)S(1)}, u32[]{:S(2)}, u32[]{:S(2)}) async-start(f32[4,16,32,128]{3,2,1,0:T(8,128)} %shard_map.148), calls=%async_computation.3 | async-start | bytes 2097152 | tf_op jit(solution)/shard_map/all_to_all | solution.py:331
  91.1 0.0 copy-start.4
  91.2 2.3 %broadcast_multiply_fusion = bf16[32,16,32,16]{3,2,1,0:T(8,128)(2,1)} fusion(bf16[16,16]{1,0:T(8,128)(2,1)S(1)} %fusion, bf16[32,32]{1,0:T(8,128)(2,1)S(1)} %copy-done.3), kind=kLoop, calls=%fused_computation | loop fusion | flops 262144 | bytes 526848 | tf_op jit(solution)/shard_map/mul | solution.py:292
  93.4 8.4 %mul.46.mix = bf16[512,512]{1,0:T(8,128)(2,1)} reshape(bf16[32,16,32,16]{3,2,1,0:T(8,128)(2,1)} %broadcast_multiply_fusion) | data formatting | bytes 1048576 | tf_op jit(solution)/shard_map/mul | solution.py:292
  101.9 0.1 broadcast_in_dim.4
  101.9 0.9 broadcast_in_dim_reshape.4.bias
  102.8 0.0 all-to-all-done.3.mixed
  102.8 1.0 copy-done
  103.8 19.0 %shard_map.149 = f32[4,16,32,128]{3,2,1,0:T(8,128)} custom-call(f32[4,16,32,128]{3,2,1,0:T(8,128)} %copy-done, bf16[512,2048]{1,0:T(8,128)(2,1)} %bitcast.11, bf16[512,2048]{1,0:T(8,128)(2,1)} %bitcast.12, bf16[512,512]{1,0:T(8,128)(2,1)} %mul.46.mix, f32[512,1]{1,0:T(8,128)} %broadcast_in_dim_reshape.4.bias, bf16[512,2048]{1,0:T(8,128)(2,1)} %constant.20.clone.cells_h, ...), custom_call_target="tpu_custom_call" | custom-call | tf_op jit(solution)/shard_map/pallas_call | solution.py:256
  122.7 14.1 %all_to_all.37.parts = f32[4,16,32,128]{3,2,1,0:T(8,128)} all-to-all(f32[4,16,32,128]{3,2,1,0:T(8,128)} %shard_map.149), channel_id=1, replica_groups=mesh['dp'=8,'azim'=16,'axial'=4] {'axial'}, dimensions={0} | all-to-all | bytes 2097152 | tf_op jit(solution)/shard_map/all_to_all | solution.py:306
  136.8 2.1 %shard_map.150 = f32[16,32,128]{2,1,0:T(8,128)} custom-call(f32[4,16,32,128]{3,2,1,0:T(8,128)} %all_to_all.37.parts, f32[4,16,128]{2,1,0:T(8,128)} %constant.26.clone.cos, f32[4,16,128]{2,1,0:T(8,128)} %constant.27.clone.sin), custom_call_target="tpu_custom_call" | custom-call | tf_op jit(solution)/shard_map/pallas_call | solution.py:256
  138.8 26.4 %all_to_all.38.refs_0_ = f32[16,32,128]{2,1,0:T(8,128)} all-to-all(f32[16,32,128]{2,1,0:T(8,128)} %shard_map.150), channel_id=1, replica_groups=mesh['dp'=8,'azim'=16,'axial'=4] {'azim'}, dimensions={0} | all-to-all | bytes 524288 | tf_op jit(solution)/shard_map/all_to_all | solution.py:308
  165.3 1.7 shard_map.151
  167.0 17.8 %all_to_all.39.pairs = f32[8,64,128]{2,1,0:T(8,128)} all-to-all(f32[8,64,128]{2,1,0:T(8,128)} %shard_map.151), channel_id=1, replica_groups=mesh['dp'=8,'azim'=16,'axial'=4] {'dp'}, dimensions={0} | all-to-all | bytes 524288 | tf_op jit(solution)/shard_map/all_to_all | solution.py:356
  184.8 3.0 %shard_map.152 = f32[2,4,16,32,32]{4,3,2,1,0:T(8,128)} custom-call(f32[8,64,128]{2,1,0:T(8,128)} %all_to_all.39.pairs), custom_call_target="tpu_custom_call" | custom-call | tf_op jit(solution)/shard_map/pallas_call | solution.py:256
  (7 shorter events, 0.0 us)
Async XLA Ops:
  9.1 36.4 %copy-start.1 = (bf16[2,1,4,16,32,32]{5,4,3,2,1,0:T(8,128)(2,1)S(1)}, bf16[2,1,4,16,32,32]{5,4,3,2,1,0:T(8,128)(2,1)}, u32[]{:S(2)}) copy-start(bf16[2,1,4,16,32,32]{5,4,3,2,1,0:T(8,128)(2,1)} %param.17) | copy-start | bytes 786436
  26.1 32.2 %all-to-all-start.1 = ((f32[16,32,128]{2,1,0:T(8,128)}), f32[16,32,128]{2,1,0:T(8,128)S(1)}, u32[]{:S(2)}, u32[]{:S(2)}) async-start(f32[16,32,128]{2,1,0:T(8,128)} %shard_map.146), calls=%async_computation.1 | async-start | bytes 524288 | tf_op jit(solution)/shard_map/all_to_all | solution.py:308
  56.5 34.6 %copy-start.3 = (bf16[32,32]{1,0:T(8,128)(2,1)S(1)}, bf16[32,32]{1,0:T(8,128)(2,1)}, u32[]{:S(2)}) copy-start(bf16[32,32]{1,0:T(8,128)(2,1)} %param.18) | copy-start | bytes 6148
  58.3 0.7 copy-start.2
  87.4 15.4 %all-to-all-start.3 = ((f32[4,16,32,128]{3,2,1,0:T(8,128)}), f32[4,16,32,128]{3,2,1,0:T(8,128)S(1)}, u32[]{:S(2)}, u32[]{:S(2)}) async-start(f32[4,16,32,128]{3,2,1,0:T(8,128)} %shard_map.148), calls=%async_computation.3 | async-start | bytes 2097152 | tf_op jit(solution)/shard_map/all_to_all | solution.py:331
  91.1 10.7 %copy-start.4 = (f32[32]{0:T(128)S(1)}, f32[32]{0:T(128)}, u32[]{:S(2)}) copy-start(f32[32]{0:T(128)} %param.19) | copy-start | bytes 388
  102.8 1.0 copy-start

commit v2 on v0

v2 whole, which is shorter than its diff:
```python
import math

import jax
import jax.numpy as jnp
import ml_dtypes
import numpy as np
from jax import lax
from jax.experimental import pallas as pl
from jax.experimental.pallas import tpu as pltpu
from jax.sharding import Mesh
from jax.sharding import PartitionSpec as P

NR = 64
NEAR = 2
BF = jnp.bfloat16
F32 = jnp.float32
FIRST_CHUNKS = 4
LAYER_CHUNKS = 4
LOCAL_CHUNKS = 2
VMEM = 40 * 1024 * 1024


def split_table(values):
    high = values.astype(ml_dtypes.bfloat16)
    low = (values - high.astype(np.float64)).astype(ml_dtypes.bfloat16)
    return high, low


def split(values):
    high = values.astype(BF)
    return high, (values - high.astype(F32)).astype(BF)


def split3(values):
    high = values.astype(BF)
    rest = values - high.astype(F32)
    mid = rest.astype(BF)
    return high, mid, (rest - mid.astype(F32)).astype(BF)


def dot(a, b):
    return lax.dot_general(a, b, (((1,), (0,)), ((), ())), preferred_element_type=F32)


def dot_nt(a, b):
    return lax.dot_general(a, b, (((1,), (1,)), ((), ())), preferred_element_type=F32)


def dot_tn(a, b):
    return lax.dot_general(a, b, (((0,), (0,)), ((), ())), preferred_element_type=F32)


class Tables:
    def __init__(self, modes, chans, cells_a, cells_l, cells_r, n_azim, n_axial):
        total_a, total_l = cells_a * n_azim, cells_l * n_axial
        k = np.arange(modes)
        radial = np.outer(k, np.arange(cells_r)) % cells_r / cells_r
        radial = radial.reshape(modes // NEAR, NEAR, cells_r).transpose(1, 0, 2).reshape(modes, cells_r)
        axial = np.outer(k, np.arange(cells_l)) % total_l / total_l
        angle = 2.0 * np.pi * (radial[:, None, None, :] + axial[None, :, :, None])
        angle = angle.reshape(modes * modes, cells_l * cells_r)
        self.cells = split_table(np.concatenate([np.cos(angle), -np.sin(angle)], 0))
        half = chans // 2
        angle = 2.0 * np.pi * np.outer(np.arange(cells_a), k) / total_a
        same = np.eye(half)

        def spread(table):
            whole = table[None, :, :, None] * same[:, None, None, :]
            return whole.reshape(half * cells_a, modes * half)

        self.turn = np.stack(split_table(spread(np.cos(angle))) + split_table(spread(np.sin(angle))))
        loc_a = modes // n_axial
        axial = (np.outer(np.arange(n_axial) * cells_l, k) % total_l / total_l).reshape(1, n_axial, modes, 1)
        azim = (np.outer(np.arange(n_azim) * cells_a, k) % total_a / total_a).reshape(n_azim, n_axial, 1, loc_a, 1)
        azim = np.broadcast_to(azim, (n_azim, n_axial, 2, loc_a, half)).reshape(n_azim, 1, 1, modes * chans)
        angle = 2.0 * np.pi * (axial + azim)
        self.place = np.stack([np.cos(angle), np.sin(angle)], 2).astype(np.float32)


def azimuth_analysis(values, turn, place, out_ref):
    cos_h, cos_l, sin_h, sin_l = (turn[i] for i in range(4))
    rows, cols = values.shape[0] // 2, values.shape[1] // 2
    near, groups, far, block, lanes = out_ref.shape
    n_kl = block // 2
    reals, imags = [], []
    for h in range(2):
        high, low = split(values[:, h * cols : (h + 1) * cols])
        by_cos = dot(high, cos_h) + dot(low, cos_h) + dot(high, cos_l)
        by_sin = dot(high, sin_h) + dot(low, sin_h) + dot(high, sin_l)
        reals.append(by_cos[:rows] + by_sin[rows:])
        imags.append(by_cos[rows:] - by_sin[:rows])
    for g in range(groups):
        at = slice(g * lanes // 2, (g + 1) * lanes // 2)
        re = jnp.concatenate([r[:, at] for r in reals], 1).reshape(near, far, n_kl, lanes)
        im = jnp.concatenate([i[:, at] for i in imags], 1).reshape(near, far, n_kl, lanes)
        to = slice(g * lanes, (g + 1) * lanes)
        c, s = place[0, :, to], place[1, :, to]
        out_ref[:, g, :, :n_kl, :] = re * c + im * s
        out_ref[:, g, :, n_kl:, :] = im * c - re * s


def azimuth_synthesis(mixed, turn, place, synth_h, synth_l):
    near, groups, far, block, lanes = mixed.shape
    n_kl = block // 2
    rows = near * far * n_kl
    reals, imags = [], []
    for g in range(groups):
        re, im = mixed[:, g, :, :n_kl, :], mixed[:, g, :, n_kl:, :]
        to = slice(g * lanes, (g + 1) * lanes)
        c, s = place[0, :, to], place[1, :, to]
        reals.append((re * c - im * s).reshape(rows, lanes))
        imags.append((im * c + re * s).reshape(rows, lanes))
    cos_h, cos_l, sin_h, sin_l = (turn[i] for i in range(4))

    def times(t_h, t_l, v):
        return dot_nt(t_h, v[0]) + dot_nt(t_h, v[1]) + dot_nt(t_l, v[0])

    half = synth_h.shape[0] // 2
    for h in range(2):
        at = slice(h * lanes // 2, (h + 1) * lanes // 2)
        re = split(jnp.concatenate([r[:, at] for r in reals], 1))
        im = split(jnp.concatenate([i[:, at] for i in imags], 1))
        real = times(cos_h, cos_l, re) - times(sin_h, sin_l, im)
        imag = times(sin_h, sin_l, re) + times(cos_h, cos_l, im)
        to = slice(h * half, (h + 1) * half)
        for q, part in enumerate((real, imag)):
            high, low = split(part)
            synth_h[to, q * rows : (q + 1) * rows] = high
            synth_l[to, q * rows : (q + 1) * rows] = low


def start_chunks(pairs, sems, chunks):
    step = pairs[0][0].shape[1] // chunks
    copies = []
    for i in range(chunks):
        at = pl.ds(i * step, step)
        copies.append([pltpu.make_async_copy(a.at[:, at], b.at[:, at], sems.at[i, j]) for j, (a, b) in enumerate(pairs)])
        for copy in copies[-1]:
            copy.start()
    return step, copies


def analysis_kernel(field, cells_h, cells_l, turn, place, out, turn_here, place_here, x, t_h, t_l, total, sems, more_sems):
    step, copies = start_chunks(((field, x), (cells_h, t_h), (cells_l, t_l)), sems, FIRST_CHUNKS)
    y = lax.axis_index("axial")
    z = lax.axis_index("zh") * NEAR + lax.axis_index("zl")
    more = [
        pltpu.make_async_copy(turn, turn_here, more_sems.at[0]),
        pltpu.make_async_copy(place.at[z, y], place_here, more_sems.at[1]),
    ]
    for copy in more:
        copy.start()
    for i in range(FIRST_CHUNKS):
        for copy in copies[i]:
            copy.wait()
        at = slice(i * step, (i + 1) * step)
        values = x[:, at]
        part = dot_nt(t_h[:, at], values) + dot_nt(t_l[:, at], values)
        total[...] = part if i == 0 else total[...] + part
    for copy in more:
        copy.wait()
    azimuth_analysis(total[...], turn_here, place_here, out)


def layer_kernel(
    mixed, turn, place, local_far, cot_far, cells_h, cells_l, out,
    synth_h, synth_l, delta_h, delta_l, local, cot, all_h, all_l, sems,
):
    pairs = ((cells_h, all_h), (cells_l, all_l), (local_far, local), (cot_far, cot))
    step, copies = start_chunks(pairs, sems, LAYER_CHUNKS)
    azimuth_synthesis(mixed, turn, place, synth_h, synth_l)
    s_h, s_l = synth_h[...], synth_l[...]
    slope = math.sqrt(2.0 / math.pi)
    for i in range(LAYER_CHUNKS):
        for copy in copies[i]:
            copy.wait()
        at = slice(i * step, (i + 1) * step)
        t_h = all_h[:, at]
        pre = dot(s_h, t_h) + dot(s_l, t_h) + dot(s_h, all_l[:, at]) + local[:, at]
        square = pre * pre
        t = jnp.tanh(pre * (slope + (slope * 0.044715) * square))
        inner = slope + (3.0 * slope * 0.044715) * square
        grad = 0.5 * (1.0 + t) + (0.5 * pre) * (1.0 - t * t) * inner
        delta_h[:, at], delta_l[:, at] = split(cot[:, at].astype(F32) * grad)
    t_h, d_h = all_h[...], delta_h[...]
    total = dot_nt(t_h, d_h) + dot_nt(t_h, delta_l[...]) + dot_nt(all_l[...], d_h)
    azimuth_analysis(total, turn, place, out)


def prepare_kernel(
    weight_far, point_far, bias_far, field, out_weight, local_far, weight, point, bias, x, local, sems, chunk_sems, out_sems
):
    small = ((point_far, point), (bias_far, bias), (weight_far, weight))
    copies = [pltpu.make_async_copy(a, b, sems.at[i]) for i, (a, b) in enumerate(small)]
    for copy in copies:
        copy.start()
    step, chunks = start_chunks(((field, x),), chunk_sems, LOCAL_CHUNKS)
    n_q, n_ka, n_kl, chans, _ = weight.shape
    rows = x.shape[0]
    cells = rows // chans

    def owner(shape, axis):
        i, c = lax.broadcasted_iota(jnp.int32, shape, axis), lax.broadcasted_iota(jnp.int32, shape, 1 - axis)
        return (i >= c * cells) & (i < (c + 1) * cells)

    left = owner((rows, chans), 0)
    right = jnp.where(owner((chans, rows), 1), 1.0, 0.0).astype(BF)
    i = lax.broadcasted_iota(jnp.int32, (rows, rows), 0)
    j = lax.broadcasted_iota(jnp.int32, (rows, rows), 1)
    copies[0].wait()
    copies[1].wait()
    wide = dot(dot(jnp.where(left, 1.0, 0.0).astype(BF), point[...]).astype(BF), right)
    mix = jnp.where(i % cells == j % cells, wide, 0.0).astype(BF)
    shift = jnp.sum(jnp.where(left, bias[...], 0.0), 1, keepdims=True)
    sends = []
    for i in range(LOCAL_CHUNKS):
        chunks[i][0].wait()
        at = slice(i * step, (i + 1) * step)
        local[:, at] = dot(mix, x[:, at]) + shift
        to = pl.ds(i * step, step)
        sends.append(pltpu.make_async_copy(local.at[:, to], local_far.at[:, to], out_sems.at[i]))
        sends[-1].start()
    half = chans // 2
    lanes = n_ka * chans
    o = lax.broadcasted_iota(jnp.int32, (chans, lanes), 0)
    lane = lax.broadcasted_iota(jnp.int32, (chans, lanes), 1)
    copies[2].wait()
    for ka in range(n_ka):
        to = jnp.where(o < half, o, o + (n_ka - 1) * half) + ka * half
        place = jnp.where(lane == to, 1.0, 0.0).astype(BF)
        for q in range(n_q):
            moved = dot(weight[q, ka].reshape(n_kl * chans, chans), place).astype(BF)
            moved = moved.reshape(n_kl, 2, half, lanes)
            for h in range(2):
                at = h * lanes // 2 + ka * half
                out_weight[:, at : at + half, q * lanes : (q + 1) * lanes] = moved[:, h]
    for copy in sends:
        copy.wait()


def mix_kernel(scale, out_scale, parts, weight, spec, out):
    far, rows, lanes = parts.shape
    n_kl = rows // 2
    total = parts[0]
    for z in range(1, far):
        total = total + parts[z]
    total = total * scale
    spec[...] = total
    stack = jnp.concatenate([*split3(total[:n_kl]), *split3(total[n_kl:])], 0)
    row = lax.broadcasted_iota(jnp.int32, (stack.shape[0], 2 * lanes), 0) % n_kl
    got = jnp.zeros((stack.shape[0], 2 * lanes), F32)
    for kl in range(n_kl):
        got = jnp.where(row == kl, dot(stack, weight[kl]), got)
    by_re = got[:n_kl] + got[n_kl : 2 * n_kl] + got[2 * n_kl : 3 * n_kl]
    by_im = got[3 * n_kl : 4 * n_kl] + got[4 * n_kl : 5 * n_kl] + got[5 * n_kl :]
    re = (by_re[:, :lanes] - by_im[:, lanes:]) * out_scale
    im = (by_re[:, lanes:] + by_im[:, :lanes]) * out_scale
    for z in range(far):
        out[z, :n_kl, :] = re
        out[z, n_kl:, :] = im


def join_kernel(scale, parts, spec, out):
    far, rows, _ = parts.shape
    total = parts[0]
    for z in range(1, far):
        total = total + parts[z]
    total = total * scale
    for d in range(out.shape[0]):
        out[d, :rows, :] = spec[...]
        out[d, rows:, :] = total


def grad_kernel(pairs, out):
    _, n_ka, n_kl, chans, _ = out.shape
    half = chans // 2
    lanes = pairs.shape[2]
    for kl in range(n_kl):
        s_re, s_im, d_re, d_im = (pairs[:, i * n_kl + kl, :] for i in range(4))
        s_h, s_l = split(jnp.concatenate([s_re, s_im], 0))
        a = jnp.concatenate([d_re, d_im], 0)
        b = jnp.concatenate([d_im, -d_re], 0)
        d_h, d_l = split(jnp.concatenate([a, b], 1))
        left = jnp.concatenate([s_h, s_l, s_h], 0)
        right = jnp.concatenate([d_h, d_h, d_l], 0)
        whole = dot_tn(left, right)
        for q in range(2):
            for ka in range(n_ka):
                for h in range(2):
                    r = h * lanes // 2 + ka * half
                    for g in range(2):
                        c = q * lanes + g * lanes // 2 + ka * half
                        out[q, ka, kl, h * half : (h + 1) * half, g * half : (g + 1) * half] = whole[r : r + half, c : c + half]


def call(kernel, out_shape, *args, **more):
    return pl.pallas_call(
        kernel,
        out_shape=out_shape,
        compiler_params=pltpu.CompilerParams(vmem_limit_bytes=VMEM),
        **more,
    )(*args)


def shape(*dims, dtype=F32):
    return jax.ShapeDtypeStruct(dims, dtype)


def per_device(field, cotangent, spectral_weight, point_weight, bias):
    _, chans, cells_a, merged = field.shape
    cells_r = NR
    cells_l = merged // cells_r
    far, n_axial, n_dp = (lax.axis_size(name) for name in ("zh", "axial", "dp"))
    n_azim = far * NEAR
    _, _, loc_a, modes, _, _ = spectral_weight.shape
    tables = Tables(modes, chans, cells_a, cells_l, cells_r, n_azim, n_axial)
    total_cells = cells_a * n_azim * cells_l * n_axial * cells_r
    forward_scale = 1.0 / math.sqrt(total_cells)
    mode_scale = 1.0 / (modes * math.sqrt(modes))
    rows_x = chans * cells_a
    rows_k = 2 * modes * modes
    lanes = loc_a * chans
    block = (2 * modes, lanes)
    whole = (NEAR, n_axial, far, *block)
    cells = [jnp.asarray(t) for t in tables.cells]
    turn, place = jnp.asarray(tables.turn), jnp.asarray(tables.place)
    x = field.reshape(rows_x, merged)
    cot = cotangent.reshape(rows_x, merged)
    near_axes = ("zl", "axial")

    def exchange(values, axes):
        flat = values.reshape(-1, *block)
        return lax.all_to_all(flat, axes, 0, 0, tiled=True).reshape(values.shape)

    def reduce(values):
        return exchange(exchange(values, near_axes).sum((0, 1)), "zh")

    far_off = pl.BlockSpec(memory_space=pl.ANY)
    near_by = pl.BlockSpec(memory_space=pltpu.VMEM)

    def stay(array):
        return pltpu.with_memory_space_constraint(array, pltpu.HBM)

    field_shape = pltpu.VMEM((rows_x, merged), BF)
    local_shape = pltpu.VMEM((rows_x, merged), F32)
    cell_shape = pltpu.VMEM((rows_k, merged), BF)
    x, cot, turn, place = map(stay, (x, cot, turn, place))
    cells = [*map(stay, cells)]
    first, turn, place = call(
        analysis_kernel,
        (pltpu.VMEM(whole, F32), pltpu.VMEM(turn.shape, BF), pltpu.VMEM(place.shape[2:], F32)),
        x,
        *cells,
        turn,
        place,
        in_specs=[far_off] * 5,
        out_specs=[near_by] * 3,
        scratch_shapes=[
            field_shape,
            cell_shape,
            cell_shape,
            pltpu.VMEM((rows_k, rows_x), F32),
            pltpu.SemaphoreType.DMA((FIRST_CHUNKS, 3)),
            pltpu.SemaphoreType.DMA((2,)),
        ],
    )
    weight_shape = spectral_weight[:, 0].shape
    weight, local = call(
        prepare_kernel,
        (pltpu.VMEM((modes, lanes, 2 * lanes), BF), pltpu.HBM((rows_x, merged), F32)),
        *map(stay, (spectral_weight[:, 0], point_weight, bias[None], x)),
        in_specs=[far_off] * 4,
        out_specs=[near_by, far_off],
        scratch_shapes=[
            pltpu.VMEM(weight_shape, BF),
            pltpu.VMEM(point_weight.shape, BF),
            pltpu.VMEM((1, chans), F32),
            field_shape,
            local_shape,
            pltpu.SemaphoreType.DMA((3,)),
            pltpu.SemaphoreType.DMA((LOCAL_CHUNKS, 1)),
            pltpu.SemaphoreType.DMA((LOCAL_CHUNKS,)),
        ],
    )
    parts = reduce(first)

    def mix_body(*refs):
        mix_kernel(forward_scale, mode_scale, *refs)

    spec, mixed = call(mix_body, (shape(*block), shape(far, *block)), parts, weight)
    mixed = exchange(mixed, "zh")
    mixed = exchange(jnp.broadcast_to(mixed, whole), near_axes)
    synth = pltpu.VMEM((rows_x, rows_k), BF)
    delta = pltpu.VMEM((rows_x, merged), BF)
    second = call(
        layer_kernel,
        pltpu.VMEM(whole, F32),
        mixed,
        turn,
        place,
        stay(local),
        cot,
        *cells,
        in_specs=[near_by] * 3 + [far_off] * 4,
        out_specs=near_by,
        scratch_shapes=[
            synth,
            synth,
            delta,
            delta,
            local_shape,
            field_shape,
            cell_shape,
            cell_shape,
            pltpu.SemaphoreType.DMA((LAYER_CHUNKS, 4)),
        ],
    )
    parts = reduce(second)

    def join_body(*refs):
        join_kernel(mode_scale, *refs)

    pairs = call(join_body, shape(n_dp, 2 * block[0], lanes), parts, spec)
    pairs = lax.all_to_all(pairs, "dp", 0, 0, tiled=True)
    grad = call(grad_kernel, shape(2, loc_a, modes, chans, chans), pairs)
    return grad[:, None]


def solution(mesh):
    n_dp, n_azim, n_axial = (mesh.shape[name] for name in ("dp", "azim", "axial"))
    fine = Mesh(mesh.devices.reshape(n_dp, n_azim // NEAR, NEAR, n_axial), ("dp", "zh", "zl", "axial"))
    azim = ("zh", "zl")
    in_specs = (
        P("dp", None, azim, "axial"),
        P("dp", None, azim, "axial"),
        P(None, azim, "axial", None, None, None),
        P(),
        P(),
    )
    out_specs = P(None, azim, "axial", None, None, None)
    return jax.shard_map(
        per_device, mesh=fine, in_specs=in_specs, out_specs=out_specs, check_vma=False
    )
```

time: 586 us -> 148 us (0.25); the launches traced: 577 us -> 148 us
  waiting for transfers between devices: 273 us -> 9.41 us
  local copies, waits for them, and re-layouts: 71.8 us -> 0.11 us
  matrix products: 69.1 us -> 0 us
  Pallas kernels: 0 us -> 26.7 us
  starting transfers between devices: 34.9 us -> 16.6 us
  blocking collectives: 109 us -> 94.1 us
  between operations: 14 us -> 0.05 us
    all_to_all x4 -> x1, waiting for transfers between devices: 192 us -> 9.41 us  [exchange(): return lax.all_to_all(flat, axes, 0, 0, tiled=True).reshape(values.shape)]
    psum x1 -> x0, waiting for transfers between devices: 80.7 us -> none  [per_device(): return lax.psum(jnp.stack([grad_re, grad_im]), 'dp')]
    dot_general x14 -> x0, matrix products: 69.1 us -> none  [the longest x1 21.1 us: per_device(): values = jnp.einsum('sorqxy,qrz->soxyz', cells, radial_inv, precision=HIGH)]
    pallas_call x0 -> x6, Pallas kernels: none -> 26.7 us  [call(): pl.pallas_call(kernel, out_shape=out_shape, compiler_params=pltpu.Compile...]
    another operation x8 -> x0, local copies, waits for them, and re-layouts: 22.4 us -> none
    reshape x9 -> x0, local copies, waits for them, and re-layouts: 20.5 us -> none  [the longest x2 9.18 us: per_device(): cells = cells.reshape(samples, chans, loc_r, 2, n_azim, cells_a * cells_l)]
    all_to_all x4 -> x1, starting transfers between devices: 34.6 us -> 16.6 us  [exchange(): return lax.all_to_all(flat, axes, 0, 0, tiled=True).reshape(values.shape)]
    all_to_all x2 -> x6, blocking collectives: 109 us -> 94.1 us  [the longest x5 75.6 us: exchange(): return lax.all_to_all(flat, axes, 0, 0, tiled=True).reshape(values.shape)]
  transfers between devices with their start and end apart: 5 -> 1, of which waited for: 5 -> 1; matrix products, arithmetic and copies ran while one was open for 0% -> 0% of each run, Pallas kernels for 0% -> 3%
where the time goes in v2:
time: 148 us
  blocking collectives  94.1 us (64%)
  Pallas kernels  26.7 us (18%)
  starting transfers between devices  16.6 us (11%)
  waiting for transfers between devices  9.41 us (6%)
    all_to_all x5, blocking collectives, exchange(): return lax.all_to_all(flat, axes, 0, 0, tiled=True).reshape(values.shape)  75.6 us
    pallas_call x6, Pallas kernels, call(): pl.pallas_call(kernel, out_shape=out_shape, compiler_params=pltpu.Compile...  26.7 us
    all_to_all x1, blocking collectives, per_device(): pairs = lax.all_to_all(pairs, 'dp', 0, 0, tiled=True)  18.4 us
    all_to_all x1, starting transfers between devices, exchange(): return lax.all_to_all(flat, axes, 0, 0, tiled=True).reshape(values.shape)  16.6 us
    all_to_all x1, waiting for transfers between devices, exchange(): return lax.all_to_all(flat, axes, 0, 0, tiled=True).reshape(values.shape)  9.41 us
  transfers between devices with their start and end apart: 1, of which 1 were waited for; matrix products, arithmetic and copies ran while one was open for 0% of the time, Pallas kernels for 3%

profile of v2, /device:TPU:1, one launch (start us, length us, event | category | flops | bytes accessed | tf_op | source)
XLA Modules:
  0.0 147.8 jit_solution(3262007577961414379)
XLA Ops:
  0.0 5.3 %shard_map.91 = (f32[2,4,8,32,128]{4,3,2,1,0:T(8,128)S(1)}, bf16[4,256,256]{2,1,0:T(8,128)(2,1)S(1)}, f32[2,16,512]{2,1,0:T(8,128)S(1)}) custom-call(bf16[512,2048]{1,0:T(8,128)(2,1)} %bitcast.16, bf16[512,2048]{1,0:T(8,128)(2,1)} %constant.10.clone.cells_h, bf16[512,2048]{1,0:T(8,128)(2,1)} %constant.11.clone.cells_l, ...), custom_call_target="tpu_custom_call" | custom-call | tf_op jit(solution)/shard_map/pallas_call | solution.py:297
  5.3 17.8 %all_to_all.35 = f32[64,32,128]{2,1,0:T(8,128)S(1)} all-to-all(f32[64,32,128]{2,1,0:T(8,128)S(1)} %bitcast.15), channel_id=1, replica_groups=mesh['dp'=8,'zh'=8,'zl'=2,'axial'=4] {'zl','axial'}, dimensions={0} | all-to-all | bytes 2097152 | tf_op jit(solution)/shard_map/all_to_all | solution.py:333
  23.1 0.7 reduce_sum.18
  23.9 16.6 %all-to-all-start.1 = ((f32[8,32,128]{2,1,0:T(8,128)}), f32[8,32,128]{2,1,0:T(8,128)S(1)}, u32[]{:S(2)}, u32[]{:S(2)}) async-start(f32[8,32,128]{2,1,0:T(8,128)} %reduce_sum.18), calls=%async_computation.1 | async-start | bytes 262144 | tf_op jit(solution)/shard_map/all_to_all | solution.py:333
  40.5 4.1 %shard_map.92 = (bf16[16,128,256]{2,1,0:T(8,128)(2,1)S(1)}, f32[512,2048]{1,0:T(8,128)}) custom-call(bf16[2,4,16,32,32]{4,3,2,1,0:T(8,128)(2,1)} %bitcast.22, bf16[32,32]{1,0:T(8,128)(2,1)} %point_far.1, f32[1,32]{1,0:T(1,128)} %bitcast.23, bf16[512,2048]{1,0:T(8,128)(2,1)} %bitcast.17), custom_call_target="tpu_custom_call" | custom-call | tf_op jit(solution)/shard_map/pallas_call | solution.py:297
  44.6 9.4 %all-to-all-done.1.refs_0_ = f32[8,32,128]{2,1,0:T(8,128)S(1)} async-done(((f32[8,32,128]{2,1,0:T(8,128)}), f32[8,32,128]{2,1,0:T(8,128)S(1)}, u32[]{:S(2)}, u32[]{:S(2)}) %all-to-all-start.1) | async-done | bytes 131104 | tf_op jit(solution)/shard_map/all_to_all | solution.py:333
  54.0 0.4 shard_map.93
  54.4 15.7 %all_to_all.36 = f32[8,32,128]{2,1,0:T(8,128)S(1)} all-to-all(f32[8,32,128]{2,1,0:T(8,128)S(1)} %get-tuple-element.14), channel_id=1, replica_groups=mesh['dp'=8,'zh'=8,'zl'=2,'axial'=4] {'zh'}, dimensions={0} | all-to-all | bytes 262144 | tf_op jit(solution)/shard_map/all_to_all | solution.py:333
  70.1 0.1 broadcast_in_dim.10
  70.2 12.8 %all_to_all.37 = f32[64,32,128]{2,1,0:T(8,128)S(1)} all-to-all(f32[64,32,128]{2,1,0:T(8,128)S(1)} %bitcast.20), channel_id=1, replica_groups=mesh['dp'=8,'zh'=8,'zl'=2,'axial'=4] {'zl','axial'}, dimensions={0} | all-to-all | bytes 2097152 | tf_op jit(solution)/shard_map/all_to_all | solution.py:333
  83.1 14.4 %shard_map.94 = f32[2,4,8,32,128]{4,3,2,1,0:T(8,128)S(1)} custom-call(f32[2,4,8,32,128]{4,3,2,1,0:T(8,128)S(1)} %bitcast.13, bf16[4,256,256]{2,1,0:T(8,128)(2,1)S(1)} %get-tuple-element.15.turn, f32[2,16,512]{2,1,0:T(8,128)S(1)} %get-tuple-element.16.place, f32[512,2048]{1,0:T(8,128)} %get-tuple-element.17.local_far, bf16[512,2048]{1,0:T(8,128)(2,1)} %bitcast.21, ...), custom_call_target="tpu_custom_call" | custom-call | tf_op jit(solution)/shard_map/pallas_call | solution.py:297
  97.5 13.7 %all_to_all.38 = f32[64,32,128]{2,1,0:T(8,128)S(1)} all-to-all(f32[64,32,128]{2,1,0:T(8,128)S(1)} %bitcast.14), channel_id=1, replica_groups=mesh['dp'=8,'zh'=8,'zl'=2,'axial'=4] {'zl','axial'}, dimensions={0} | all-to-all | bytes 2097152 | tf_op jit(solution)/shard_map/all_to_all | solution.py:333
  111.1 0.1 reduce_sum.19
  111.2 15.6 %all_to_all.39.refs_0_ = f32[8,32,128]{2,1,0:T(8,128)S(1)} all-to-all(f32[8,32,128]{2,1,0:T(8,128)S(1)} %reduce_sum.19), channel_id=1, replica_groups=mesh['dp'=8,'zh'=8,'zl'=2,'axial'=4] {'zh'}, dimensions={0} | all-to-all | bytes 262144 | tf_op jit(solution)/shard_map/all_to_all | solution.py:333
  126.8 18.4 %all_to_all.40.pairs = f32[8,64,128]{2,1,0:T(8,128)S(1)} all-to-all(f32[8,64,128]{2,1,0:T(8,128)S(1)} %shard_map.95), channel_id=1, replica_groups=mesh['dp'=8,'zh'=8,'zl'=2,'axial'=4] {'dp'}, dimensions={0} | all-to-all | bytes 524288 | tf_op jit(solution)/shard_map/all_to_all | solution.py:424
  145.3 2.6 %shard_map.96 = f32[2,4,16,32,32]{4,3,2,1,0:T(8,128)} custom-call(f32[8,64,128]{2,1,0:T(8,128)S(1)} %all_to_all.40.pairs), custom_call_target="tpu_custom_call" | custom-call | tf_op jit(solution)/shard_map/pallas_call | solution.py:297
  (1 shorter events, 0.0 us)
Async XLA Ops:
  23.9 30.1 %all-to-all-start.1 = ((f32[8,32,128]{2,1,0:T(8,128)}), f32[8,32,128]{2,1,0:T(8,128)S(1)}, u32[]{:S(2)}, u32[]{:S(2)}) async-start(f32[8,32,128]{2,1,0:T(8,128)} %reduce_sum.18), calls=%async_computation.1 | async-start | bytes 262144 | tf_op jit(solution)/shard_map/all_to_all | solution.py:333

commit v3 on v2

--- a/solution.py
+++ b/solution.py
@@ -14,8 +14,7 @@
 NEAR = 2
 BF = jnp.bfloat16
 F32 = jnp.float32
-FIRST_CHUNKS = 4
-LAYER_CHUNKS = 4
+GROUPS = 4
 LOCAL_CHUNKS = 2
 VMEM = 40 * 1024 * 1024
 
@@ -56,10 +55,15 @@
         k = np.arange(modes)
         radial = np.outer(k, np.arange(cells_r)) % cells_r / cells_r
         radial = radial.reshape(modes // NEAR, NEAR, cells_r).transpose(1, 0, 2).reshape(modes, cells_r)
-        axial = np.outer(k, np.arange(cells_l)) % total_l / total_l
+        group_l = cells_l // GROUPS
+        axial = np.outer(k, np.arange(group_l)) % total_l / total_l
         angle = 2.0 * np.pi * (radial[:, None, None, :] + axial[None, :, :, None])
-        angle = angle.reshape(modes * modes, cells_l * cells_r)
-        self.cells = split_table(np.concatenate([np.cos(angle), -np.sin(angle)], 0))
+        angle = angle.reshape(modes * modes, group_l * cells_r)
+        self.cells = np.stack(split_table(np.concatenate([np.cos(angle), -np.sin(angle)], 0)))
+        angle = 2.0 * np.pi * (np.outer(np.arange(GROUPS) * group_l, k) % total_l / total_l)
+        both = np.stack([np.cos(angle), np.sin(angle)], 1).astype(np.float32)
+        self.rows = np.repeat(both[:, :, :, None], 128, 3)
+        self.cols = np.tile(both, (1, 1, modes))[:, :, None, :]
         half = chans // 2
         angle = 2.0 * np.pi * np.outer(np.arange(cells_a), k) / total_a
         same = np.eye(half)
@@ -99,7 +103,7 @@
         out_ref[:, g, :, n_kl:, :] = im * c - re * s
 
 
-def azimuth_synthesis(mixed, turn, place, synth_h, synth_l):
+def azimuth_synthesis(mixed, turn, place, synth):
     near, groups, far, block, lanes = mixed.shape
     n_kl = block // 2
     rows = near * far * n_kl
@@ -115,75 +119,122 @@
     def times(t_h, t_l, v):
         return dot_nt(t_h, v[0]) + dot_nt(t_h, v[1]) + dot_nt(t_l, v[0])
 
-    half = synth_h.shape[0] // 2
+    half = synth.shape[0] // 2
     for h in range(2):
         at = slice(h * lanes // 2, (h + 1) * lanes // 2)
         re = split(jnp.concatenate([r[:, at] for r in reals], 1))
         im = split(jnp.concatenate([i[:, at] for i in imags], 1))
         real = times(cos_h, cos_l, re) - times(sin_h, sin_l, im)
         imag = times(sin_h, sin_l, re) + times(cos_h, cos_l, im)
-        to = slice(h * half, (h + 1) * half)
-        for q, part in enumerate((real, imag)):
-            high, low = split(part)
-            synth_h[to, q * rows : (q + 1) * rows] = high
-            synth_l[to, q * rows : (q + 1) * rows] = low
-
-
-def start_chunks(pairs, sems, chunks):
-    step = pairs[0][0].shape[1] // chunks
-    copies = []
-    for i in range(chunks):
-        at = pl.ds(i * step, step)
-        copies.append([pltpu.make_async_copy(a.at[:, at], b.at[:, at], sems.at[i, j]) for j, (a, b) in enumerate(pairs)])
-        for copy in copies[-1]:
-            copy.start()
-    return step, copies
-
-
-def analysis_kernel(field, cells_h, cells_l, turn, place, out, turn_here, place_here, x, t_h, t_l, total, sems, more_sems):
-    step, copies = start_chunks(((field, x), (cells_h, t_h), (cells_l, t_l)), sems, FIRST_CHUNKS)
+        synth[h * half : (h + 1) * half, :rows] = real
+        synth[h * half : (h + 1) * half, rows:] = imag
+
+
+def add_group(total, part, group, rows):
+    if group == 0:
+        return part
+    half, cols = part.shape[0] // 2, part.shape[1]
+    n_kl = rows.shape[2]
+    re, im = part[:half].reshape(-1, n_kl, cols), part[half:].reshape(-1, n_kl, cols)
+    c, s = rows[group, 0][:, :1], rows[group, 1][:, :1]
+    turned = jnp.concatenate([re * c + im * s, im * c - re * s], 0)
+    return total + turned.reshape(part.shape)
+
+
+def turn_group(values, group, cols):
+    if group == 0:
+        return split(values)
+    half = values.shape[1] // 2
+    re, im = values[:, :half], values[:, half:]
+    c, s = cols[group, 0], cols[group, 1]
+    return split(jnp.concatenate([re * c - im * s, im * c + re * s], 1))
+
+
+def start_columns(source, target, sems, widths):
+    step = source.shape[1] // sum(widths)
+    copies, at = [], 0
+    for i, width in enumerate(widths):
+        columns = pl.ds(at * step, width * step)
+        copies.append(pltpu.make_async_copy(source.at[:, columns], target.at[:, columns], sems.at[i]))
+        copies[-1].start()
+        at += width
+    return copies
+
+
+def analysis_kernel(
+    field, cells, turn, place, rows, cols, out, cells_here, turn_here, place_here, rows_here, cols_here, x, sems, more_sems
+):
     y = lax.axis_index("axial")
     z = lax.axis_index("zh") * NEAR + lax.axis_index("zl")
-    more = [
-        pltpu.make_async_copy(turn, turn_here, more_sems.at[0]),
-        pltpu.make_async_copy(place.at[z, y], place_here, more_sems.at[1]),
-    ]
-    for copy in more:
+    pairs = (
+        (cells.at[0], cells_here.at[0]),
+        (cells.at[1], cells_here.at[1]),
+        (rows, rows_here),
+        (turn, turn_here),
+        (place.at[z, y], place_here),
+        (cols, cols_here),
+    )
+    more = [pltpu.make_async_copy(a, b, more_sems.at[i]) for i, (a, b) in enumerate(pairs)]
+    for copy in more[:3]:
         copy.start()
-    for i in range(FIRST_CHUNKS):
-        for copy in copies[i]:
-            copy.wait()
-        at = slice(i * step, (i + 1) * step)
-        values = x[:, at]
-        part = dot_nt(t_h[:, at], values) + dot_nt(t_l[:, at], values)
-        total[...] = part if i == 0 else total[...] + part
-    for copy in more:
+    first, rest = start_columns(field, x, sems, (1, GROUPS - 1))
+    for copy in more[3:]:
+        copy.start()
+    step = x.shape[1] // GROUPS
+    total = None
+    for copy in (first, *more[:3]):
         copy.wait()
-    azimuth_analysis(total[...], turn_here, place_here, out)
+    for g in range(GROUPS):
+        if g == 1:
+            for copy in (rest, *more[3:]):
+                copy.wait()
+        values = x[:, g * step : (g + 1) * step]
+        part = dot_nt(cells_here[0], values) + dot_nt(cells_here[1], values)
+        total = add_group(total, part, g, rows_here)
+    azimuth_analysis(total, turn_here, place_here, out)
 
 
 def layer_kernel(
-    mixed, turn, place, local_far, cot_far, cells_h, cells_l, out,
-    synth_h, synth_l, delta_h, delta_l, local, cot, all_h, all_l, sems,
+    mixed, cells, turn, place, rows, cols, local_far, cot_far, out, synth, pre, delta_h, delta_l, local, cot, sems
 ):
-    pairs = ((cells_h, all_h), (cells_l, all_l), (local_far, local), (cot_far, cot))
-    step, copies = start_chunks(pairs, sems, LAYER_CHUNKS)
-    azimuth_synthesis(mixed, turn, place, synth_h, synth_l)
-    s_h, s_l = synth_h[...], synth_l[...]
+    copies = [pltpu.make_async_copy(local_far, local, sems.at[0]), pltpu.make_async_copy(cot_far, cot, sems.at[1])]
+    for copy in copies:
+        copy.start()
+    azimuth_synthesis(mixed, turn, place, synth)
+    step = local.shape[1] // GROUPS
     slope = math.sqrt(2.0 / math.pi)
-    for i in range(LAYER_CHUNKS):
-        for copy in copies[i]:
-            copy.wait()
-        at = slice(i * step, (i + 1) * step)
-        t_h = all_h[:, at]
-        pre = dot(s_h, t_h) + dot(s_l, t_h) + dot(s_h, all_l[:, at]) + local[:, at]
-        square = pre * pre
-        t = jnp.tanh(pre * (slope + (slope * 0.044715) * square))
+
+    def synthesize(g):
+        high, low = turn_group(synth[...], g, cols)
+        pre[g] = dot(high, cells[0]) + dot(low, cells[0]) + dot(high, cells[1])
+
+    def activate(g):
+        at = slice(g * step, (g + 1) * step)
+        value = pre[g] + local[:, at]
+        square = value * value
+        t = jnp.tanh(value * (slope + (slope * 0.044715) * square))
         inner = slope + (3.0 * slope * 0.044715) * square
-        grad = 0.5 * (1.0 + t) + (0.5 * pre) * (1.0 - t * t) * inner
-        delta_h[:, at], delta_l[:, at] = split(cot[:, at].astype(F32) * grad)
-    t_h, d_h = all_h[...], delta_h[...]
-    total = dot_nt(t_h, d_h) + dot_nt(t_h, delta_l[...]) + dot_nt(all_l[...], d_h)
+        grad = 0.5 * (1.0 + t) + (0.5 * value) * (1.0 - t * t) * inner
+        delta_h[g], delta_l[g] = split(cot[:, at].astype(F32) * grad)
+
+    def analyze(g, total):
+        high = delta_h[g]
+        part = dot_nt(cells[0], high) + dot_nt(cells[0], delta_l[g]) + dot_nt(cells[1], high)
+        return add_group(total, part, g, rows)
+
+    ahead = 2
+    for g in range(ahead):
+        synthesize(g)
+    for copy in copies:
+        copy.wait()
+    total = None
+    for g in range(GROUPS):
+        if ahead <= g + 1 < GROUPS:
+            synthesize(g + 1)
+        activate(g)
+        if g > 0:
+            total = analyze(g - 1, total)
+    total = analyze(GROUPS - 1, total)
     azimuth_analysis(total, turn, place, out)
 
 
@@ -194,7 +245,8 @@
     copies = [pltpu.make_async_copy(a, b, sems.at[i]) for i, (a, b) in enumerate(small)]
     for copy in copies:
         copy.start()
-    step, chunks = start_chunks(((field, x),), chunk_sems, LOCAL_CHUNKS)
+    chunks = start_columns(field, x, chunk_sems, (1,) * LOCAL_CHUNKS)
+    step = x.shape[1] // LOCAL_CHUNKS
     n_q, n_ka, n_kl, chans, _ = weight.shape
     rows = x.shape[0]
     cells = rows // chans
@@ -214,7 +266,7 @@
     shift = jnp.sum(jnp.where(left, bias[...], 0.0), 1, keepdims=True)
     sends = []
     for i in range(LOCAL_CHUNKS):
-        chunks[i][0].wait()
+        chunks[i].wait()
         at = slice(i * step, (i + 1) * step)
         local[:, at] = dot(mix, x[:, at]) + shift
         to = pl.ds(i * step, step)
@@ -271,10 +323,12 @@
         out[d, rows:, :] = total
 
 
-def grad_kernel(pairs, out):
+def grad_kernel(pairs, out_far, out, sems):
     _, n_ka, n_kl, chans, _ = out.shape
     half = chans // 2
     lanes = pairs.shape[2]
+    copies = []
+    part = n_kl // sems.shape[0]
     for kl in range(n_kl):
         s_re, s_im, d_re, d_im = (pairs[:, i * n_kl + kl, :] for i in range(4))
         s_h, s_l = split(jnp.concatenate([s_re, s_im], 0))
@@ -291,6 +345,12 @@
                     for g in range(2):
                         c = q * lanes + g * lanes // 2 + ka * half
                         out[q, ka, kl, h * half : (h + 1) * half, g * half : (g + 1) * half] = whole[r : r + half, c : c + half]
+        if kl % part == part - 1:
+            at = pl.ds(kl + 1 - part, part)
+            copies.append(pltpu.make_async_copy(out.at[:, :, at], out_far.at[:, :, at], sems.at[kl // part]))
+            copies[-1].start()
+    for copy in copies:
+        copy.wait()
 
 
 def call(kernel, out_shape, *args, **more):
@@ -322,8 +382,7 @@
     lanes = loc_a * chans
     block = (2 * modes, lanes)
     whole = (NEAR, n_axial, far, *block)
-    cells = [jnp.asarray(t) for t in tables.cells]
-    turn, place = jnp.asarray(tables.turn), jnp.asarray(tables.place)
+    held = [jnp.asarray(t) for t in (tables.cells, tables.turn, tables.place, tables.rows, tables.cols)]
     x = field.reshape(rows_x, merged)
     cot = cotangent.reshape(rows_x, merged)
     near_axes = ("zl", "axial")
@@ -343,25 +402,19 @@
 
     field_shape = pltpu.VMEM((rows_x, merged), BF)
     local_shape = pltpu.VMEM((rows_x, merged), F32)
-    cell_shape = pltpu.VMEM((rows_k, merged), BF)
-    x, cot, turn, place = map(stay, (x, cot, turn, place))
-    cells = [*map(stay, cells)]
-    first, turn, place = call(
+    x, cot, *held = map(stay, (x, cot, *held))
+    held_shapes = [pltpu.VMEM(t.shape[2:] if i == 2 else t.shape, t.dtype) for i, t in enumerate(held)]
+    first, *held = call(
         analysis_kernel,
-        (pltpu.VMEM(whole, F32), pltpu.VMEM(turn.shape, BF), pltpu.VMEM(place.shape[2:], F32)),
+        (pltpu.VMEM(whole, F32), *held_shapes),
         x,
-        *cells,
-        turn,
-        place,
-        in_specs=[far_off] * 5,
-        out_specs=[near_by] * 3,
+        *held,
+        in_specs=[far_off] * 6,
+        out_specs=[near_by] * 6,
         scratch_shapes=[
             field_shape,
-            cell_shape,
-            cell_shape,
-            pltpu.VMEM((rows_k, rows_x), F32),
-            pltpu.SemaphoreType.DMA((FIRST_CHUNKS, 3)),
             pltpu.SemaphoreType.DMA((2,)),
+            pltpu.SemaphoreType.DMA((6,)),
         ],
     )
     weight_shape = spectral_weight[:, 0].shape
@@ -378,7 +431,7 @@
             field_shape,
             local_shape,
             pltpu.SemaphoreType.DMA((3,)),
-            pltpu.SemaphoreType.DMA((LOCAL_CHUNKS, 1)),
+            pltpu.SemaphoreType.DMA((LOCAL_CHUNKS,)),
             pltpu.SemaphoreType.DMA((LOCAL_CHUNKS,)),
         ],
     )
@@ -390,29 +443,24 @@
     spec, mixed = call(mix_body, (shape(*block), shape(far, *block)), parts, weight)
     mixed = exchange(mixed, "zh")
     mixed = exchange(jnp.broadcast_to(mixed, whole), near_axes)
-    synth = pltpu.VMEM((rows_x, rows_k), BF)
-    delta = pltpu.VMEM((rows_x, merged), BF)
+    group = (GROUPS, rows_x, merged // GROUPS)
     second = call(
         layer_kernel,
         pltpu.VMEM(whole, F32),
         mixed,
-        turn,
-        place,
+        *held,
         stay(local),
         cot,
-        *cells,
-        in_specs=[near_by] * 3 + [far_off] * 4,
+        in_specs=[near_by] * 6 + [far_off] * 2,
         out_specs=near_by,
         scratch_shapes=[
-            synth,
-            synth,
-            delta,
-            delta,
+            pltpu.VMEM((rows_x, rows_k), F32),
+            pltpu.VMEM(group, F32),
+            pltpu.VMEM(group, BF),
+            pltpu.VMEM(group, BF),
             local_shape,
             field_shape,
-            cell_shape,
-            cell_shape,
-            pltpu.SemaphoreType.DMA((LAYER_CHUNKS, 4)),
+            pltpu.SemaphoreType.DMA((2,)),
         ],
     )
     parts = reduce(second)
@@ -422,7 +470,15 @@
 
     pairs = call(join_body, shape(n_dp, 2 * block[0], lanes), parts, spec)
     pairs = lax.all_to_all(pairs, "dp", 0, 0, tiled=True)
-    grad = call(grad_kernel, shape(2, loc_a, modes, chans, chans), pairs)
+    grad_dims = (2, loc_a, modes, chans, chans)
+    grad = call(
+        grad_kernel,
+        pltpu.HBM(grad_dims, F32),
+        pairs,
+        in_specs=[near_by],
+        out_specs=far_off,
+        scratch_shapes=[pltpu.VMEM(grad_dims, F32), pltpu.SemaphoreType.DMA((4,))],
+    )
     return grad[:, None]
 
 

time: 148 us -> 144 us (0.973)
  Pallas kernels: 26.7 us -> 22.3 us
    pallas_call x6, Pallas kernels: 26.7 us -> 22.3 us  [call(): pl.pallas_call(kernel, out_shape=out_shape, compiler_params=pltpu.Compile...]
where the time goes in v3:
time: 144 us; the launch traced here: 143 us
  blocking collectives  93.9 us (65%)
  Pallas kernels  22.3 us (15%)
  starting transfers between devices  16.6 us (12%)
  waiting for transfers between devices  9.41 us (7%)
    all_to_all x5, blocking collectives, exchange(): return lax.all_to_all(flat, axes, 0, 0, tiled=True).reshape(values.shape)  75.6 us
    pallas_call x6, Pallas kernels, call(): pl.pallas_call(kernel, out_shape=out_shape, compiler_params=pltpu.Compile...  22.3 us
    all_to_all x1, blocking collectives, per_device(): pairs = lax.all_to_all(pairs, 'dp', 0, 0, tiled=True)  18.3 us
    all_to_all x1, starting transfers between devices, exchange(): return lax.all_to_all(flat, axes, 0, 0, tiled=True).reshape(values.shape)  16.6 us
    all_to_all x1, waiting for transfers between devices, exchange(): return lax.all_to_all(flat, axes, 0, 0, tiled=True).reshape(values.shape)  9.41 us
  transfers between devices with their start and end apart: 1, of which 1 were waited for; matrix products, arithmetic and copies ran while one was open for 0% of the time, Pallas kernels for 3%

profile of v3, /device:TPU:1, one launch (start us, length us, event | category | flops | bytes accessed | tf_op | source)
XLA Modules:
  0.0 143.3 jit_solution(2187973410359730264)
XLA Ops:
  0.0 5.6 %shard_map.100 = (f32[2,4,8,32,128]{4,3,2,1,0:T(8,128)S(1)}, bf16[2,512,512]{2,1,0:T(8,128)(2,1)S(1)}, bf16[4,256,256]{2,1,0:T(8,128)(2,1)S(1)}, f32[2,16,512]{2...) custom-call(bf16[512,2048]{1,0:T(8,128)(2,1)} %bitcast.16, ...), custom_call_target="tpu_custom_call" | custom-call | tf_op jit(solution)/shard_map/pallas_call | solution.py:357
  5.6 17.8 %all_to_all.35 = f32[64,32,128]{2,1,0:T(8,128)S(1)} all-to-all(f32[64,32,128]{2,1,0:T(8,128)S(1)} %bitcast.15), channel_id=1, replica_groups=mesh['dp'=8,'zh'=8,'zl'=2,'axial'=4] {'zl','axial'}, dimensions={0} | all-to-all | bytes 2097152 | tf_op jit(solution)/shard_map/all_to_all | solution.py:392
  23.3 0.7 reduce_sum.18
  24.1 16.6 %all-to-all-start.1 = ((f32[8,32,128]{2,1,0:T(8,128)}), f32[8,32,128]{2,1,0:T(8,128)S(1)}, u32[]{:S(2)}, u32[]{:S(2)}) async-start(f32[8,32,128]{2,1,0:T(8,128)} %reduce_sum.18), calls=%async_computation.1 | async-start | bytes 262144 | tf_op jit(solution)/shard_map/all_to_all | solution.py:392
  40.7 4.1 %shard_map.101 = (bf16[16,128,256]{2,1,0:T(8,128)(2,1)S(1)}, f32[512,2048]{1,0:T(8,128)}) custom-call(bf16[2,4,16,32,32]{4,3,2,1,0:T(8,128)(2,1)} %bitcast.22, bf16[32,32]{1,0:T(8,128)(2,1)} %point_far.1, f32[1,32]{1,0:T(1,128)} %bitcast.23, bf16[512,2048]{1,0:T(8,128)(2,1)} %bitcast.17), custom_call_target="tpu_custom_call" | custom-call | tf_op jit(solution)/shard_map/pallas_call | solution.py:357
  44.8 9.4 %all-to-all-done.1.refs_0_ = f32[8,32,128]{2,1,0:T(8,128)S(1)} async-done(((f32[8,32,128]{2,1,0:T(8,128)}), f32[8,32,128]{2,1,0:T(8,128)S(1)}, u32[]{:S(2)}, u32[]{:S(2)}) %all-to-all-start.1) | async-done | bytes 131104 | tf_op jit(solution)/shard_map/all_to_all | solution.py:392
  54.2 0.4 shard_map.102
  54.6 15.7 %all_to_all.36 = f32[8,32,128]{2,1,0:T(8,128)S(1)} all-to-all(f32[8,32,128]{2,1,0:T(8,128)S(1)} %get-tuple-element.17), channel_id=1, replica_groups=mesh['dp'=8,'zh'=8,'zl'=2,'axial'=4] {'zh'}, dimensions={0} | all-to-all | bytes 262144 | tf_op jit(solution)/shard_map/all_to_all | solution.py:392
  70.3 0.1 broadcast_in_dim.10
  70.4 12.8 %all_to_all.37 = f32[64,32,128]{2,1,0:T(8,128)S(1)} all-to-all(f32[64,32,128]{2,1,0:T(8,128)S(1)} %bitcast.20), channel_id=1, replica_groups=mesh['dp'=8,'zh'=8,'zl'=2,'axial'=4] {'zl','axial'}, dimensions={0} | all-to-all | bytes 2097152 | tf_op jit(solution)/shard_map/all_to_all | solution.py:392
  83.3 10.1 %shard_map.103 = f32[2,4,8,32,128]{4,3,2,1,0:T(8,128)S(1)} custom-call(f32[2,4,8,32,128]{4,3,2,1,0:T(8,128)S(1)} %bitcast.13, bf16[2,512,512]{2,1,0:T(8,128)(2,1)S(1)} %get-tuple-element.18.cells, bf16[4,256,256]{2,1,0:T(8,128)(2,1)S(1)} %get-tuple-element.19.turn, f32[2,16,512]{2,1,0:T(8,128)S(1)} %get-tuple-element.20.place, ...), custom_call_target="tpu_custom_call" | custom-call | tf_op jit(solution)/shard_map/pallas_call | solution.py:357
  93.4 13.7 %all_to_all.38 = f32[64,32,128]{2,1,0:T(8,128)S(1)} all-to-all(f32[64,32,128]{2,1,0:T(8,128)S(1)} %bitcast.14), channel_id=1, replica_groups=mesh['dp'=8,'zh'=8,'zl'=2,'axial'=4] {'zl','axial'}, dimensions={0} | all-to-all | bytes 2097152 | tf_op jit(solution)/shard_map/all_to_all | solution.py:392
  107.1 0.1 reduce_sum.19
  107.1 15.6 %all_to_all.39.refs_0_ = f32[8,32,128]{2,1,0:T(8,128)S(1)} all-to-all(f32[8,32,128]{2,1,0:T(8,128)S(1)} %reduce_sum.19), channel_id=1, replica_groups=mesh['dp'=8,'zh'=8,'zl'=2,'axial'=4] {'zh'}, dimensions={0} | all-to-all | bytes 262144 | tf_op jit(solution)/shard_map/all_to_all | solution.py:392
  122.8 18.3 %all_to_all.40.pairs = f32[8,64,128]{2,1,0:T(8,128)S(1)} all-to-all(f32[8,64,128]{2,1,0:T(8,128)S(1)} %shard_map.104), channel_id=1, replica_groups=mesh['dp'=8,'zh'=8,'zl'=2,'axial'=4] {'dp'}, dimensions={0} | all-to-all | bytes 524288 | tf_op jit(solution)/shard_map/all_to_all | solution.py:472
  141.1 2.1 %shard_map.105 = f32[2,4,16,32,32]{4,3,2,1,0:T(8,128)} custom-call(f32[8,64,128]{2,1,0:T(8,128)S(1)} %all_to_all.40.pairs), custom_call_target="tpu_custom_call" | custom-call | tf_op jit(solution)/shard_map/pallas_call | solution.py:357
  (1 shorter events, 0.0 us)
Async XLA Ops:
  24.1 30.1 %all-to-all-start.1 = ((f32[8,32,128]{2,1,0:T(8,128)}), f32[8,32,128]{2,1,0:T(8,128)S(1)}, u32[]{:S(2)}, u32[]{:S(2)}) async-start(f32[8,32,128]{2,1,0:T(8,128)} %reduce_sum.18), calls=%async_computation.1 | async-start | bytes 262144 | tf_op jit(solution)/shard_map/all_to_all | solution.py:392

commit v4 on v3

--- a/solution.py
+++ b/solution.py
@@ -15,8 +15,7 @@
 BF = jnp.bfloat16
 F32 = jnp.float32
 GROUPS = 4
-LOCAL_CHUNKS = 2
-VMEM = 40 * 1024 * 1024
+VMEM = 32 * 1024 * 1024
 
 
 def split_table(values):
@@ -162,11 +161,14 @@
 
 
 def analysis_kernel(
-    field, cells, turn, place, rows, cols, out, cells_here, turn_here, place_here, rows_here, cols_here, x, sems, more_sems
+    field, cells, turn, place, rows, cols, point_far, bias_far,
+    out, cells_here, turn_here, place_here, rows_here, cols_here, out_mix, out_bias, x, point, bias, sems, more_sems,
 ):
     y = lax.axis_index("axial")
     z = lax.axis_index("zh") * NEAR + lax.axis_index("zl")
     pairs = (
+        (point_far, point),
+        (bias_far, bias),
         (cells.at[0], cells_here.at[0]),
         (cells.at[1], cells_here.at[1]),
         (rows, rows_here),
@@ -175,18 +177,21 @@
         (cols, cols_here),
     )
     more = [pltpu.make_async_copy(a, b, more_sems.at[i]) for i, (a, b) in enumerate(pairs)]
-    for copy in more[:3]:
+    for copy in more[:5]:
         copy.start()
     first, rest = start_columns(field, x, sems, (1, GROUPS - 1))
-    for copy in more[3:]:
+    for copy in more[5:]:
         copy.start()
     step = x.shape[1] // GROUPS
     total = None
-    for copy in (first, *more[:3]):
+    for copy in more[:2]:
+        copy.wait()
+    spread_rows(point, bias, out_mix, out_bias)
+    for copy in (first, *more[2:5]):
         copy.wait()
     for g in range(GROUPS):
         if g == 1:
-            for copy in (rest, *more[3:]):
+            for copy in (rest, *more[5:]):
                 copy.wait()
         values = x[:, g * step : (g + 1) * step]
         part = dot_nt(cells_here[0], values) + dot_nt(cells_here[1], values)
@@ -195,13 +200,14 @@
 
 
 def layer_kernel(
-    mixed, cells, turn, place, rows, cols, local_far, cot_far, out, synth, pre, delta_h, delta_l, local, cot, sems
+    mixed, cells, turn, place, rows, cols, mix, bias, field, cot_far, out, synth, pre, delta_h, delta_l, x, cot, sems
 ):
-    copies = [pltpu.make_async_copy(local_far, local, sems.at[0]), pltpu.make_async_copy(cot_far, cot, sems.at[1])]
+    copies = [pltpu.make_async_copy(field, x, sems.at[0]), pltpu.make_async_copy(cot_far, cot, sems.at[1])]
     for copy in copies:
         copy.start()
     azimuth_synthesis(mixed, turn, place, synth)
-    step = local.shape[1] // GROUPS
+    step = x.shape[1] // GROUPS
+    shift = jnp.concatenate([bias[...]] * (step // bias.shape[1]), 1)
     slope = math.sqrt(2.0 / math.pi)
 
     def synthesize(g):
@@ -210,7 +216,7 @@
 
     def activate(g):
         at = slice(g * step, (g + 1) * step)
-        value = pre[g] + local[:, at]
+        value = pre[g] + dot(mix[...], x[:, at]) + shift
         square = value * value
         t = jnp.tanh(value * (slope + (slope * 0.044715) * square))
         inner = slope + (3.0 * slope * 0.044715) * square
@@ -238,17 +244,8 @@
     azimuth_analysis(total, turn, place, out)
 
 
-def prepare_kernel(
-    weight_far, point_far, bias_far, field, out_weight, local_far, weight, point, bias, x, local, sems, chunk_sems, out_sems
-):
-    small = ((point_far, point), (bias_far, bias), (weight_far, weight))
-    copies = [pltpu.make_async_copy(a, b, sems.at[i]) for i, (a, b) in enumerate(small)]
-    for copy in copies:
-        copy.start()
-    chunks = start_columns(field, x, chunk_sems, (1,) * LOCAL_CHUNKS)
-    step = x.shape[1] // LOCAL_CHUNKS
-    n_q, n_ka, n_kl, chans, _ = weight.shape
-    rows = x.shape[0]
+def spread_rows(point, bias, out_mix, out_bias):
+    chans, rows = point.shape[0], out_mix.shape[0]
     cells = rows // chans
 
     def owner(shape, axis):
@@ -257,26 +254,20 @@
 
     left = owner((rows, chans), 0)
     right = jnp.where(owner((chans, rows), 1), 1.0, 0.0).astype(BF)
+    wide = dot(dot(jnp.where(left, 1.0, 0.0).astype(BF), point[...]).astype(BF), right)
     i = lax.broadcasted_iota(jnp.int32, (rows, rows), 0)
     j = lax.broadcasted_iota(jnp.int32, (rows, rows), 1)
-    copies[0].wait()
-    copies[1].wait()
-    wide = dot(dot(jnp.where(left, 1.0, 0.0).astype(BF), point[...]).astype(BF), right)
-    mix = jnp.where(i % cells == j % cells, wide, 0.0).astype(BF)
-    shift = jnp.sum(jnp.where(left, bias[...], 0.0), 1, keepdims=True)
-    sends = []
-    for i in range(LOCAL_CHUNKS):
-        chunks[i].wait()
-        at = slice(i * step, (i + 1) * step)
-        local[:, at] = dot(mix, x[:, at]) + shift
-        to = pl.ds(i * step, step)
-        sends.append(pltpu.make_async_copy(local.at[:, to], local_far.at[:, to], out_sems.at[i]))
-        sends[-1].start()
+    out_mix[...] = jnp.where(i % cells == j % cells, wide, 0.0).astype(BF)
+    column = jnp.sum(jnp.where(left, bias[...], 0.0), 1, keepdims=True)
+    out_bias[...] = jnp.broadcast_to(column, out_bias.shape)
+
+
+def pack_weights(weight, out):
+    n_q, n_ka, n_kl, chans, _ = weight.shape
     half = chans // 2
     lanes = n_ka * chans
     o = lax.broadcasted_iota(jnp.int32, (chans, lanes), 0)
     lane = lax.broadcasted_iota(jnp.int32, (chans, lanes), 1)
-    copies[2].wait()
     for ka in range(n_ka):
         to = jnp.where(o < half, o, o + (n_ka - 1) * half) + ka * half
         place = jnp.where(lane == to, 1.0, 0.0).astype(BF)
@@ -285,12 +276,20 @@
             moved = moved.reshape(n_kl, 2, half, lanes)
             for h in range(2):
                 at = h * lanes // 2 + ka * half
-                out_weight[:, at : at + half, q * lanes : (q + 1) * lanes] = moved[:, h]
-    for copy in sends:
-        copy.wait()
-
-
-def mix_kernel(scale, out_scale, parts, weight, spec, out):
+                out[:, at : at + half, q * lanes : (q + 1) * lanes] = moved[:, h]
+
+
+def sum_kernel(parts, out):
+    near, groups, *_ = parts.shape
+    total = None
+    for place in range(near * groups):
+        part = parts[place // groups, place % groups]
+        total = part if total is None else total + part
+    out[...] = total
+
+
+def mix_kernel(scale, out_scale, parts, raw, spec, out, weight):
+    pack_weights(raw, weight)
     far, rows, lanes = parts.shape
     n_kl = rows // 2
     total = parts[0]
@@ -392,7 +391,7 @@
         return lax.all_to_all(flat, axes, 0, 0, tiled=True).reshape(values.shape)
 
     def reduce(values):
-        return exchange(exchange(values, near_axes).sum((0, 1)), "zh")
+        return exchange(call(sum_kernel, pltpu.VMEM((far, *block), F32), exchange(values, near_axes)), "zh")
 
     far_off = pl.BlockSpec(memory_space=pl.ANY)
     near_by = pl.BlockSpec(memory_space=pltpu.VMEM)
@@ -401,38 +400,23 @@
         return pltpu.with_memory_space_constraint(array, pltpu.HBM)
 
     field_shape = pltpu.VMEM((rows_x, merged), BF)
-    local_shape = pltpu.VMEM((rows_x, merged), F32)
     x, cot, *held = map(stay, (x, cot, *held))
     held_shapes = [pltpu.VMEM(t.shape[2:] if i == 2 else t.shape, t.dtype) for i, t in enumerate(held)]
     first, *held = call(
         analysis_kernel,
-        (pltpu.VMEM(whole, F32), *held_shapes),
+        (pltpu.VMEM(whole, F32), *held_shapes, pltpu.VMEM((rows_x, rows_x), BF), pltpu.VMEM((rows_x, 128), F32)),
         x,
         *held,
-        in_specs=[far_off] * 6,
-        out_specs=[near_by] * 6,
+        stay(point_weight),
+        stay(bias[None]),
+        in_specs=[far_off] * 8,
+        out_specs=[near_by] * 8,
         scratch_shapes=[
             field_shape,
-            pltpu.SemaphoreType.DMA((2,)),
-            pltpu.SemaphoreType.DMA((6,)),
-        ],
-    )
-    weight_shape = spectral_weight[:, 0].shape
-    weight, local = call(
-        prepare_kernel,
-        (pltpu.VMEM((modes, lanes, 2 * lanes), BF), pltpu.HBM((rows_x, merged), F32)),
-        *map(stay, (spectral_weight[:, 0], point_weight, bias[None], x)),
-        in_specs=[far_off] * 4,
-        out_specs=[near_by, far_off],
-        scratch_shapes=[
-            pltpu.VMEM(weight_shape, BF),
             pltpu.VMEM(point_weight.shape, BF),
             pltpu.VMEM((1, chans), F32),
-            field_shape,
-            local_shape,
-            pltpu.SemaphoreType.DMA((3,)),
-            pltpu.SemaphoreType.DMA((LOCAL_CHUNKS,)),
-            pltpu.SemaphoreType.DMA((LOCAL_CHUNKS,)),
+            pltpu.SemaphoreType.DMA((2,)),
+            pltpu.SemaphoreType.DMA((8,)),
         ],
     )
     parts = reduce(first)
@@ -440,7 +424,13 @@
     def mix_body(*refs):
         mix_kernel(forward_scale, mode_scale, *refs)
 
-    spec, mixed = call(mix_body, (shape(*block), shape(far, *block)), parts, weight)
+    spec, mixed = call(
+        mix_body,
+        (shape(*block), shape(far, *block)),
+        parts,
+        spectral_weight[:, 0],
+        scratch_shapes=[pltpu.VMEM((modes, lanes, 2 * lanes), BF)],
+    )
     mixed = exchange(mixed, "zh")
     mixed = exchange(jnp.broadcast_to(mixed, whole), near_axes)
     group = (GROUPS, rows_x, merged // GROUPS)
@@ -449,16 +439,16 @@
         pltpu.VMEM(whole, F32),
         mixed,
         *held,
-        stay(local),
+        x,
         cot,
-        in_specs=[near_by] * 6 + [far_off] * 2,
+        in_specs=[near_by] * 8 + [far_off] * 2,
         out_specs=near_by,
         scratch_shapes=[
             pltpu.VMEM((rows_x, rows_k), F32),
             pltpu.VMEM(group, F32),
             pltpu.VMEM(group, BF),
             pltpu.VMEM(group, BF),
-            local_shape,
+            field_shape,
             field_shape,
             pltpu.SemaphoreType.DMA((2,)),
         ],

time: 144 us -> 145 us (level)
  blocking collectives: 93.9 us -> 124 us
  starting transfers between devices: 16.6 us -> 0 us
  waiting for transfers between devices: 9.41 us -> 0 us
  Pallas kernels: 22.3 us -> 19.9 us
    all_to_all x5 -> x6, blocking collectives: 75.6 us -> 106 us  [exchange(): return lax.all_to_all(flat, axes, 0, 0, tiled=True).reshape(values.shape)]
    all_to_all x1 -> x0, starting transfers between devices: 16.6 us -> none  [exchange(): return lax.all_to_all(flat, axes, 0, 0, tiled=True).reshape(values.shape)]
    all_to_all x1 -> x0, waiting for transfers between devices: 9.41 us -> none  [exchange(): return lax.all_to_all(flat, axes, 0, 0, tiled=True).reshape(values.shape)]
    pallas_call x6 -> x7, Pallas kernels: 22.3 us -> 19.9 us  [call(): pl.pallas_call(kernel, out_shape=out_shape, compiler_params=pltpu.Compile...]
  transfers between devices with their start and end apart: 1 -> 0, of which waited for: 1 -> 0; matrix products, arithmetic and copies ran while one was open for 0% -> 0% of each run, Pallas kernels for 3% -> 0%
where the time goes in v4:
time: 145 us; the launch traced here: 144 us
  blocking collectives  124 us (86%)
  Pallas kernels  19.9 us (14%)
    all_to_all x6, blocking collectives, exchange(): return lax.all_to_all(flat, axes, 0, 0, tiled=True).reshape(values.shape)  106 us
    pallas_call x7, Pallas kernels, call(): pl.pallas_call(kernel, out_shape=out_shape, compiler_params=pltpu.Compile...  19.9 us
    all_to_all x1, blocking collectives, per_device(): pairs = lax.all_to_all(pairs, 'dp', 0, 0, tiled=True)  18.3 us

profile of v4, /device:TPU:1, one launch (start us, length us, event | category | flops | bytes accessed | tf_op | source)
XLA Modules:
  0.0 144.2 jit_solution(2914490268489390980)
XLA Ops:
  0.0 5.6 %shard_map.100 = (f32[2,4,8,32,128]{4,3,2,1,0:T(8,128)S(1)}, bf16[2,512,512]{2,1,0:T(8,128)(2,1)S(1)}, bf16[4,256,256]{2,1,0:T(8,128)(2,1)S(1)}, f32[2,16,512]{2...) custom-call(bf16[512,2048]{1,0:T(8,128)(2,1)} %bitcast.19, ...), custom_call_target="tpu_custom_call" | custom-call | tf_op jit(solution)/shard_map/pallas_call | solution.py:356
  5.7 0.0 copy-start
  5.7 17.9 %all_to_all.35 = f32[64,32,128]{2,1,0:T(8,128)S(1)} all-to-all(f32[64,32,128]{2,1,0:T(8,128)S(1)} %bitcast.18), channel_id=1, replica_groups=mesh['dp'=8,'zh'=8,'zl'=2,'axial'=4] {'zl','axial'}, dimensions={0} | all-to-all | bytes 2097152 | tf_op jit(solution)/shard_map/all_to_all | solution.py:391
  23.6 0.1 shard_map.101
  23.6 29.9 %all_to_all.36.refs_0_ = f32[8,32,128]{2,1,0:T(8,128)S(1)} all-to-all(f32[8,32,128]{2,1,0:T(8,128)S(1)} %shard_map.101), channel_id=1, replica_groups=mesh['dp'=8,'zh'=8,'zl'=2,'axial'=4] {'zh'}, dimensions={0} | all-to-all | bytes 262144 | tf_op jit(solution)/shard_map/all_to_all | solution.py:391
  53.5 0.0 copy-done
  53.6 0.7 shard_map.102
  54.3 15.7 %all_to_all.37 = f32[8,32,128]{2,1,0:T(8,128)S(1)} all-to-all(f32[8,32,128]{2,1,0:T(8,128)S(1)} %get-tuple-element.16), channel_id=1, replica_groups=mesh['dp'=8,'zh'=8,'zl'=2,'axial'=4] {'zh'}, dimensions={0} | all-to-all | bytes 262144 | tf_op jit(solution)/shard_map/all_to_all | solution.py:391
  70.0 0.1 broadcast_in_dim.10
  70.1 12.8 %all_to_all.38 = f32[64,32,128]{2,1,0:T(8,128)S(1)} all-to-all(f32[64,32,128]{2,1,0:T(8,128)S(1)} %bitcast.21), channel_id=1, replica_groups=mesh['dp'=8,'zh'=8,'zl'=2,'axial'=4] {'zl','axial'}, dimensions={0} | all-to-all | bytes 2097152 | tf_op jit(solution)/shard_map/all_to_all | solution.py:391
  83.0 11.3 %shard_map.103 = f32[2,4,8,32,128]{4,3,2,1,0:T(8,128)S(1)} custom-call(f32[2,4,8,32,128]{4,3,2,1,0:T(8,128)S(1)} %bitcast.13, bf16[2,512,512]{2,1,0:T(8,128)(2,1)S(1)} %get-tuple-element.17.cells, bf16[4,256,256]{2,1,0:T(8,128)(2,1)S(1)} %get-tuple-element.18.turn, f32[2,16,512]{2,1,0:T(8,128)S(1)} %get-tuple-element.19.place, ...), custom_call_target="tpu_custom_call" | custom-call | tf_op jit(solution)/shard_map/pallas_call | solution.py:356
  94.3 13.6 %all_to_all.39 = f32[64,32,128]{2,1,0:T(8,128)S(1)} all-to-all(f32[64,32,128]{2,1,0:T(8,128)S(1)} %bitcast.14), channel_id=1, replica_groups=mesh['dp'=8,'zh'=8,'zl'=2,'axial'=4] {'zl','axial'}, dimensions={0} | all-to-all | bytes 2097152 | tf_op jit(solution)/shard_map/all_to_all | solution.py:391
  108.0 0.1 shard_map.104
  108.0 15.6 %all_to_all.40.refs_0_ = f32[8,32,128]{2,1,0:T(8,128)S(1)} all-to-all(f32[8,32,128]{2,1,0:T(8,128)S(1)} %shard_map.104), channel_id=1, replica_groups=mesh['dp'=8,'zh'=8,'zl'=2,'axial'=4] {'zh'}, dimensions={0} | all-to-all | bytes 262144 | tf_op jit(solution)/shard_map/all_to_all | solution.py:391
  123.6 18.3 %all_to_all.41.pairs = f32[8,64,128]{2,1,0:T(8,128)S(1)} all-to-all(f32[8,64,128]{2,1,0:T(8,128)S(1)} %shard_map.105), channel_id=1, replica_groups=mesh['dp'=8,'zh'=8,'zl'=2,'axial'=4] {'dp'}, dimensions={0} | all-to-all | bytes 524288 | tf_op jit(solution)/shard_map/all_to_all | solution.py:462
  142.0 2.1 %shard_map.106 = f32[2,4,16,32,32]{4,3,2,1,0:T(8,128)} custom-call(f32[8,64,128]{2,1,0:T(8,128)S(1)} %all_to_all.41.pairs), custom_call_target="tpu_custom_call" | custom-call | tf_op jit(solution)/shard_map/pallas_call | solution.py:356
  (1 shorter events, 0.0 us)
Async XLA Ops:
  5.7 47.9 %copy-start = (bf16[2,1,4,16,32,32]{5,4,3,2,1,0:T(8,128)(2,1)S(1)}, bf16[2,1,4,16,32,32]{5,4,3,2,1,0:T(8,128)(2,1)}, u32[]{:S(2)}) copy-start(bf16[2,1,4,16,32,32]{5,4,3,2,1,0:T(8,128)(2,1)} %param.12) | copy-start | bytes 786436

commit v5 on v4

--- a/solution.py
+++ b/solution.py
@@ -59,10 +59,13 @@
         angle = 2.0 * np.pi * (radial[:, None, None, :] + axial[None, :, :, None])
         angle = angle.reshape(modes * modes, group_l * cells_r)
         self.cells = np.stack(split_table(np.concatenate([np.cos(angle), -np.sin(angle)], 0)))
+        order = np.arange(group_l).reshape(-1, 2, 2).transpose(0, 2, 1).reshape(-1)
+        parted = self.cells.reshape(2, 2, NEAR, modes * modes // NEAR, group_l, 2, cells_r // 2)[..., order, 0, :]
+        self.halves = parted.transpose(0, 2, 1, 3, 4, 5).reshape(2, NEAR, 2 * modes * modes // NEAR, group_l * cells_r // 2)
         angle = 2.0 * np.pi * (np.outer(np.arange(GROUPS) * group_l, k) % total_l / total_l)
         both = np.stack([np.cos(angle), np.sin(angle)], 1).astype(np.float32)
         self.rows = np.repeat(both[:, :, :, None], 128, 3)
-        self.cols = np.tile(both, (1, 1, modes))[:, :, None, :]
+        self.cols = np.tile(both, (1, 1, modes // NEAR))[:, :, None, :]
         half = chans // 2
         angle = 2.0 * np.pi * np.outer(np.arange(cells_a), k) / total_a
         same = np.eye(half)
@@ -149,6 +152,24 @@
     return split(jnp.concatenate([re * c - im * s, im * c + re * s], 1))
 
 
+def first_half():
+    return lax.broadcasted_iota(jnp.int32, (1, 128), 1) % NR < NR // 2
+
+
+def fold(values):
+    a, b = values[:, :128], values[:, 128:]
+    u = jnp.where(first_half(), a, pltpu.roll(b, NR // 2, 1))
+    v = jnp.where(first_half(), pltpu.roll(a, 128 - NR // 2, 1), b)
+    return u + v, u - v
+
+
+def unfold(even, odd):
+    u, v = even + odd, even - odd
+    a = jnp.where(first_half(), u, pltpu.roll(v, NR // 2, 1))
+    b = jnp.where(first_half(), pltpu.roll(u, 128 - NR // 2, 1), v)
+    return a, b
+
+
 def start_columns(source, target, sems, widths):
     step = source.shape[1] // sum(widths)
     copies, at = [], 0
@@ -161,8 +182,8 @@
 
 
 def analysis_kernel(
-    field, cells, turn, place, rows, cols, point_far, bias_far,
-    out, cells_here, turn_here, place_here, rows_here, cols_here, out_mix, out_bias, x, point, bias, sems, more_sems,
+    field, halves, turn, place, rows, cols, cells, point_far, bias_far,
+    out, halves_here, turn_here, place_here, rows_here, cols_here, out_mix, out_bias, x, cells_here, point, bias, sems, more_sems,
 ):
     y = lax.axis_index("axial")
     z = lax.axis_index("zh") * NEAR + lax.axis_index("zl")
@@ -175,6 +196,7 @@
         (turn, turn_here),
         (place.at[z, y], place_here),
         (cols, cols_here),
+        (halves, halves_here),
     )
     more = [pltpu.make_async_copy(a, b, more_sems.at[i]) for i, (a, b) in enumerate(pairs)]
     for copy in more[:5]:
@@ -200,7 +222,7 @@
 
 
 def layer_kernel(
-    mixed, cells, turn, place, rows, cols, mix, bias, field, cot_far, out, synth, pre, delta_h, delta_l, x, cot, sems
+    mixed, halves, turn, place, rows, cols, mix, bias, field, cot_far, out, synth, pre, delta_h, delta_l, x, cot, sems
 ):
     copies = [pltpu.make_async_copy(field, x, sems.at[0]), pltpu.make_async_copy(cot_far, cot, sems.at[1])]
     for copy in copies:
@@ -210,9 +232,19 @@
     shift = jnp.concatenate([bias[...]] * (step // bias.shape[1]), 1)
     slope = math.sqrt(2.0 / math.pi)
 
+    half = synth.shape[1] // 2
+    part = half // NEAR
+
     def synthesize(g):
-        high, low = turn_group(synth[...], g, cols)
-        pre[g] = dot(high, cells[0]) + dot(low, cells[0]) + dot(high, cells[1])
+        sums = []
+        for p in range(NEAR):
+            at = [synth[:, q * half + p * part : q * half + (p + 1) * part] for q in range(2)]
+            high, low = turn_group(jnp.concatenate(at, 1), g, cols)
+            sums.append(dot(high, halves[0, p]) + dot(low, halves[0, p]) + dot(high, halves[1, p]))
+        for j in range(step // 256):
+            a, b = unfold(*(value[:, j * 128 : (j + 1) * 128] for value in sums))
+            pre[g, :, j * 256 : j * 256 + 128] = a
+            pre[g, :, j * 256 + 128 : (j + 1) * 256] = b
 
     def activate(g):
         at = slice(g * step, (g + 1) * step)
@@ -221,26 +253,35 @@
         t = jnp.tanh(value * (slope + (slope * 0.044715) * square))
         inner = slope + (3.0 * slope * 0.044715) * square
         grad = 0.5 * (1.0 + t) + (0.5 * value) * (1.0 - t * t) * inner
-        delta_h[g], delta_l[g] = split(cot[:, at].astype(F32) * grad)
-
-    def analyze(g, total):
-        high = delta_h[g]
-        part = dot_nt(cells[0], high) + dot_nt(cells[0], delta_l[g]) + dot_nt(cells[1], high)
-        return add_group(total, part, g, rows)
+        delta = cot[:, at].astype(F32) * grad
+        for j in range(step // 256):
+            to = slice(j * 128, (j + 1) * 128)
+            for p, value in enumerate(fold(delta[:, j * 256 : (j + 1) * 256])):
+                delta_h[g, p, :, to], delta_l[g, p, :, to] = split(value)
+
+    def analyze(g, totals):
+        out = []
+        for p in range(NEAR):
+            high = delta_h[g, p]
+            both = dot_nt(halves[:, p].reshape(2 * half, -1), high)
+            value = both[:half] + both[half:] + dot_nt(halves[0, p], delta_l[g, p])
+            out.append(add_group(totals[p], value, g, rows))
+        return out
 
     ahead = 2
     for g in range(ahead):
         synthesize(g)
     for copy in copies:
         copy.wait()
-    total = None
+    totals = [None] * NEAR
     for g in range(GROUPS):
         if ahead <= g + 1 < GROUPS:
             synthesize(g + 1)
         activate(g)
         if g > 0:
-            total = analyze(g - 1, total)
-    total = analyze(GROUPS - 1, total)
+            totals = analyze(g - 1, totals)
+    totals = analyze(GROUPS - 1, totals)
+    total = jnp.concatenate([value[q * part : (q + 1) * part] for q in range(2) for value in totals], 0)
     azimuth_analysis(total, turn, place, out)
 
 
@@ -381,7 +422,8 @@
     lanes = loc_a * chans
     block = (2 * modes, lanes)
     whole = (NEAR, n_axial, far, *block)
-    held = [jnp.asarray(t) for t in (tables.cells, tables.turn, tables.place, tables.rows, tables.cols)]
+    held = [jnp.asarray(t) for t in (tables.halves, tables.turn, tables.place, tables.rows, tables.cols)]
+    cells = jnp.asarray(tables.cells)
     x = field.reshape(rows_x, merged)
     cot = cotangent.reshape(rows_x, merged)
     near_axes = ("zl", "axial")
@@ -407,16 +449,16 @@
         (pltpu.VMEM(whole, F32), *held_shapes, pltpu.VMEM((rows_x, rows_x), BF), pltpu.VMEM((rows_x, 128), F32)),
         x,
         *held,
-        stay(point_weight),
-        stay(bias[None]),
-        in_specs=[far_off] * 8,
+        *map(stay, (cells, point_weight, bias[None])),
+        in_specs=[far_off] * 9,
         out_specs=[near_by] * 8,
         scratch_shapes=[
             field_shape,
+            pltpu.VMEM(cells.shape, BF),
             pltpu.VMEM(point_weight.shape, BF),
             pltpu.VMEM((1, chans), F32),
             pltpu.SemaphoreType.DMA((2,)),
-            pltpu.SemaphoreType.DMA((8,)),
+            pltpu.SemaphoreType.DMA((9,)),
         ],
     )
     parts = reduce(first)
@@ -434,6 +476,7 @@
     mixed = exchange(mixed, "zh")
     mixed = exchange(jnp.broadcast_to(mixed, whole), near_axes)
     group = (GROUPS, rows_x, merged // GROUPS)
+    folded = (GROUPS, NEAR, rows_x, merged // GROUPS // NEAR)
     second = call(
         layer_kernel,
         pltpu.VMEM(whole, F32),
@@ -446,8 +489,8 @@
         scratch_shapes=[
             pltpu.VMEM((rows_x, rows_k), F32),
             pltpu.VMEM(group, F32),
-            pltpu.VMEM(group, BF),
-            pltpu.VMEM(group, BF),
+            pltpu.VMEM(folded, BF),
+            pltpu.VMEM(folded, BF),
             field_shape,
             field_shape,
             pltpu.SemaphoreType.DMA((2,)),

time: 145 us -> 143 us (0.986)
  no operation moved by 1% of the time
where the time goes in v5:
time: 143 us
  blocking collectives  124 us (87%)
  Pallas kernels  18.6 us (13%)
    all_to_all x6, blocking collectives, exchange(): return lax.all_to_all(flat, axes, 0, 0, tiled=True).reshape(values.shape)  106 us
    pallas_call x7, Pallas kernels, call(): pl.pallas_call(kernel, out_shape=out_shape, compiler_params=pltpu.Compile...  18.6 us
    all_to_all x1, blocking collectives, per_device(): pairs = lax.all_to_all(pairs, 'dp', 0, 0, tiled=True)  18.3 us

profile of v5, /device:TPU:1, one launch (start us, length us, event | category | flops | bytes accessed | tf_op | source)
XLA Modules:
  0.0 142.9 jit_solution(9891738395412981017)
XLA Ops:
  0.0 5.6 %shard_map.109 = (f32[2,4,8,32,128]{4,3,2,1,0:T(8,128)S(1)}, bf16[2,2,256,256]{3,2,1,0:T(8,128)(2,1)S(1)}, bf16[4,256,256]{2,1,0:T(8,128)(2,1)S(1)}, f32[2,16,51...) custom-call(bf16[512,2048]{1,0:T(8,128)(2,1)} %bitcast.19, ...), custom_call_target="tpu_custom_call" | custom-call | tf_op jit(solution)/shard_map/pallas_call | solution.py:397
  5.7 0.0 copy-start
  5.7 17.9 %all_to_all.35 = f32[64,32,128]{2,1,0:T(8,128)S(1)} all-to-all(f32[64,32,128]{2,1,0:T(8,128)S(1)} %bitcast.18), channel_id=1, replica_groups=mesh['dp'=8,'zh'=8,'zl'=2,'axial'=4] {'zl','axial'}, dimensions={0} | all-to-all | bytes 2097152 | tf_op jit(solution)/shard_map/all_to_all | solution.py:433
  23.6 0.1 shard_map.110
  23.6 29.9 %all_to_all.36.refs_0_ = f32[8,32,128]{2,1,0:T(8,128)S(1)} all-to-all(f32[8,32,128]{2,1,0:T(8,128)S(1)} %shard_map.110), channel_id=1, replica_groups=mesh['dp'=8,'zh'=8,'zl'=2,'axial'=4] {'zh'}, dimensions={0} | all-to-all | bytes 262144 | tf_op jit(solution)/shard_map/all_to_all | solution.py:433
  53.6 0.0 copy-done
  53.6 0.7 shard_map.111
  54.3 15.7 %all_to_all.37 = f32[8,32,128]{2,1,0:T(8,128)S(1)} all-to-all(f32[8,32,128]{2,1,0:T(8,128)S(1)} %get-tuple-element.16), channel_id=1, replica_groups=mesh['dp'=8,'zh'=8,'zl'=2,'axial'=4] {'zh'}, dimensions={0} | all-to-all | bytes 262144 | tf_op jit(solution)/shard_map/all_to_all | solution.py:433
  70.0 0.1 broadcast_in_dim.10
  70.1 12.8 %all_to_all.38 = f32[64,32,128]{2,1,0:T(8,128)S(1)} all-to-all(f32[64,32,128]{2,1,0:T(8,128)S(1)} %bitcast.21), channel_id=1, replica_groups=mesh['dp'=8,'zh'=8,'zl'=2,'axial'=4] {'zl','axial'}, dimensions={0} | all-to-all | bytes 2097152 | tf_op jit(solution)/shard_map/all_to_all | solution.py:433
  83.0 10.0 %shard_map.112 = f32[2,4,8,32,128]{4,3,2,1,0:T(8,128)S(1)} custom-call(f32[2,4,8,32,128]{4,3,2,1,0:T(8,128)S(1)} %bitcast.13, bf16[2,2,256,256]{3,2,1,0:T(8,128)(2,1)S(1)} %get-tuple-element.17.halves, bf16[4,256,256]{2,1,0:T(8,128)(2,1)S(1)} %get-tuple-element.18.turn, f32[2,16,512]{2,1,0:T(8,128)S(1)} %get-tuple-element.19.place, ...), custom_call_target="tpu_custom_call" | custom-call | tf_op jit(solution)/shard_map/pallas_call | solution.py:397
  93.0 13.7 %all_to_all.39 = f32[64,32,128]{2,1,0:T(8,128)S(1)} all-to-all(f32[64,32,128]{2,1,0:T(8,128)S(1)} %bitcast.14), channel_id=1, replica_groups=mesh['dp'=8,'zh'=8,'zl'=2,'axial'=4] {'zl','axial'}, dimensions={0} | all-to-all | bytes 2097152 | tf_op jit(solution)/shard_map/all_to_all | solution.py:433
  106.6 0.1 shard_map.113
  106.7 15.6 %all_to_all.40.refs_0_ = f32[8,32,128]{2,1,0:T(8,128)S(1)} all-to-all(f32[8,32,128]{2,1,0:T(8,128)S(1)} %shard_map.113), channel_id=1, replica_groups=mesh['dp'=8,'zh'=8,'zl'=2,'axial'=4] {'zh'}, dimensions={0} | all-to-all | bytes 262144 | tf_op jit(solution)/shard_map/all_to_all | solution.py:433
  122.3 18.3 %all_to_all.41.pairs = f32[8,64,128]{2,1,0:T(8,128)S(1)} all-to-all(f32[8,64,128]{2,1,0:T(8,128)S(1)} %shard_map.114), channel_id=1, replica_groups=mesh['dp'=8,'zh'=8,'zl'=2,'axial'=4] {'dp'}, dimensions={0} | all-to-all | bytes 524288 | tf_op jit(solution)/shard_map/all_to_all | solution.py:505
  140.6 2.1 %shard_map.115 = f32[2,4,16,32,32]{4,3,2,1,0:T(8,128)} custom-call(f32[8,64,128]{2,1,0:T(8,128)S(1)} %all_to_all.41.pairs), custom_call_target="tpu_custom_call" | custom-call | tf_op jit(solution)/shard_map/pallas_call | solution.py:397
  (1 shorter events, 0.0 us)
Async XLA Ops:
  5.7 47.9 %copy-start = (bf16[2,1,4,16,32,32]{5,4,3,2,1,0:T(8,128)(2,1)S(1)}, bf16[2,1,4,16,32,32]{5,4,3,2,1,0:T(8,128)(2,1)}, u32[]{:S(2)}) copy-start(bf16[2,1,4,16,32,32]{5,4,3,2,1,0:T(8,128)(2,1)} %param.13) | copy-start | bytes 786436

commit v6 on v5

--- a/solution.py
+++ b/solution.py
@@ -58,9 +58,9 @@
         axial = np.outer(k, np.arange(group_l)) % total_l / total_l
         angle = 2.0 * np.pi * (radial[:, None, None, :] + axial[None, :, :, None])
         angle = angle.reshape(modes * modes, group_l * cells_r)
-        self.cells = np.stack(split_table(np.concatenate([np.cos(angle), -np.sin(angle)], 0)))
+        cells = np.stack(split_table(np.concatenate([np.cos(angle), -np.sin(angle)], 0)))
         order = np.arange(group_l).reshape(-1, 2, 2).transpose(0, 2, 1).reshape(-1)
-        parted = self.cells.reshape(2, 2, NEAR, modes * modes // NEAR, group_l, 2, cells_r // 2)[..., order, 0, :]
+        parted = cells.reshape(2, 2, NEAR, modes * modes // NEAR, group_l, 2, cells_r // 2)[..., order, 0, :]
         self.halves = parted.transpose(0, 2, 1, 3, 4, 5).reshape(2, NEAR, 2 * modes * modes // NEAR, group_l * cells_r // 2)
         angle = 2.0 * np.pi * (np.outer(np.arange(GROUPS) * group_l, k) % total_l / total_l)
         both = np.stack([np.cos(angle), np.sin(angle)], 1).astype(np.float32)
@@ -170,6 +170,21 @@
     return a, b
 
 
+def add_halves(totals, parts, group, halves, rows):
+    out = []
+    for p, (high, low) in enumerate(parts):
+        both = dot_nt(halves[:, p].reshape(-1, halves.shape[3]), high)
+        half = both.shape[0] // 2
+        value = both[:half] + both[half:] + dot_nt(halves[0, p], low)
+        out.append(add_group(totals[p], value, group, rows))
+    return out
+
+
+def join_halves(totals):
+    part = totals[0].shape[0] // 2
+    return jnp.concatenate([value[q * part : (q + 1) * part] for q in range(2) for value in totals], 0)
+
+
 def start_columns(source, target, sems, widths):
     step = source.shape[1] // sum(widths)
     copies, at = [], 0
@@ -182,43 +197,42 @@
 
 
 def analysis_kernel(
-    field, halves, turn, place, rows, cols, cells, point_far, bias_far,
-    out, halves_here, turn_here, place_here, rows_here, cols_here, out_mix, out_bias, x, cells_here, point, bias, sems, more_sems,
+    field, halves, turn, place, rows, cols, point_far, bias_far,
+    out, halves_here, turn_here, place_here, rows_here, cols_here, out_mix, out_bias, x, point, bias, sems, more_sems,
 ):
     y = lax.axis_index("axial")
     z = lax.axis_index("zh") * NEAR + lax.axis_index("zl")
     pairs = (
         (point_far, point),
         (bias_far, bias),
-        (cells.at[0], cells_here.at[0]),
-        (cells.at[1], cells_here.at[1]),
+        (halves, halves_here),
         (rows, rows_here),
         (turn, turn_here),
         (place.at[z, y], place_here),
         (cols, cols_here),
-        (halves, halves_here),
     )
     more = [pltpu.make_async_copy(a, b, more_sems.at[i]) for i, (a, b) in enumerate(pairs)]
-    for copy in more[:5]:
+    for copy in more[:4]:
         copy.start()
     first, rest = start_columns(field, x, sems, (1, GROUPS - 1))
-    for copy in more[5:]:
+    for copy in more[4:]:
         copy.start()
     step = x.shape[1] // GROUPS
-    total = None
     for copy in more[:2]:
         copy.wait()
     spread_rows(point, bias, out_mix, out_bias)
-    for copy in (first, *more[2:5]):
+    for copy in (first, *more[2:4]):
         copy.wait()
+    totals = [None] * NEAR
     for g in range(GROUPS):
         if g == 1:
-            for copy in (rest, *more[5:]):
+            for copy in (rest, *more[4:]):
                 copy.wait()
-        values = x[:, g * step : (g + 1) * step]
-        part = dot_nt(cells_here[0], values) + dot_nt(cells_here[1], values)
-        total = add_group(total, part, g, rows_here)
-    azimuth_analysis(total, turn_here, place_here, out)
+        values = x[:, g * step : (g + 1) * step].astype(F32)
+        folded = zip(*(fold(values[:, j * 256 : (j + 1) * 256]) for j in range(step // 256)))
+        parts = [split(jnp.concatenate(value, 1)) for value in folded]
+        totals = add_halves(totals, parts, g, halves_here, rows_here)
+    azimuth_analysis(join_halves(totals), turn_here, place_here, out)
 
 
 def layer_kernel(
@@ -251,22 +265,17 @@
         value = pre[g] + dot(mix[...], x[:, at]) + shift
         square = value * value
         t = jnp.tanh(value * (slope + (slope * 0.044715) * square))
-        inner = slope + (3.0 * slope * 0.044715) * square
-        grad = 0.5 * (1.0 + t) + (0.5 * value) * (1.0 - t * t) * inner
-        delta = cot[:, at].astype(F32) * grad
+        inner = value * (slope + (3.0 * slope * 0.044715) * square)
+        share = 0.5 + 0.5 * t
+        delta = cot[:, at].astype(F32) * (share + share * (inner - inner * t))
         for j in range(step // 256):
             to = slice(j * 128, (j + 1) * 128)
             for p, value in enumerate(fold(delta[:, j * 256 : (j + 1) * 256])):
                 delta_h[g, p, :, to], delta_l[g, p, :, to] = split(value)
 
     def analyze(g, totals):
-        out = []
-        for p in range(NEAR):
-            high = delta_h[g, p]
-            both = dot_nt(halves[:, p].reshape(2 * half, -1), high)
-            value = both[:half] + both[half:] + dot_nt(halves[0, p], delta_l[g, p])
-            out.append(add_group(totals[p], value, g, rows))
-        return out
+        parts = [(delta_h[g, p], delta_l[g, p]) for p in range(NEAR)]
+        return add_halves(totals, parts, g, halves, rows)
 
     ahead = 2
     for g in range(ahead):
@@ -281,8 +290,7 @@
         if g > 0:
             totals = analyze(g - 1, totals)
     totals = analyze(GROUPS - 1, totals)
-    total = jnp.concatenate([value[q * part : (q + 1) * part] for q in range(2) for value in totals], 0)
-    azimuth_analysis(total, turn, place, out)
+    azimuth_analysis(join_halves(totals), turn, place, out)
 
 
 def spread_rows(point, bias, out_mix, out_bias):
@@ -423,7 +431,6 @@
     block = (2 * modes, lanes)
     whole = (NEAR, n_axial, far, *block)
     held = [jnp.asarray(t) for t in (tables.halves, tables.turn, tables.place, tables.rows, tables.cols)]
-    cells = jnp.asarray(tables.cells)
     x = field.reshape(rows_x, merged)
     cot = cotangent.reshape(rows_x, merged)
     near_axes = ("zl", "axial")
@@ -449,16 +456,15 @@
         (pltpu.VMEM(whole, F32), *held_shapes, pltpu.VMEM((rows_x, rows_x), BF), pltpu.VMEM((rows_x, 128), F32)),
         x,
         *held,
-        *map(stay, (cells, point_weight, bias[None])),
-        in_specs=[far_off] * 9,
+        *map(stay, (point_weight, bias[None])),
+        in_specs=[far_off] * 8,
         out_specs=[near_by] * 8,
         scratch_shapes=[
             field_shape,
-            pltpu.VMEM(cells.shape, BF),
             pltpu.VMEM(point_weight.shape, BF),
             pltpu.VMEM((1, chans), F32),
             pltpu.SemaphoreType.DMA((2,)),
-            pltpu.SemaphoreType.DMA((9,)),
+            pltpu.SemaphoreType.DMA((7,)),
         ],
     )
     parts = reduce(first)

time: 143 us -> 143 us (level)
  no operation moved by 1% of the time
where the time goes in v6:
time: 143 us
  blocking collectives  124 us (87%)
  Pallas kernels  18.3 us (13%)
    all_to_all x6, blocking collectives, exchange(): return lax.all_to_all(flat, axes, 0, 0, tiled=True).reshape(values.shape)  106 us
    pallas_call x7, Pallas kernels, call(): pl.pallas_call(kernel, out_shape=out_shape, compiler_params=pltpu.Compile...  18.3 us
    all_to_all x1, blocking collectives, per_device(): pairs = lax.all_to_all(pairs, 'dp', 0, 0, tiled=True)  18.3 us

profile of v6, /device:TPU:1, one launch (start us, length us, event | category | flops | bytes accessed | tf_op | source)
XLA Modules:
  0.0 142.6 jit_solution(15123924951474568527)
XLA Ops:
  0.0 5.5 %shard_map.100 = (f32[2,4,8,32,128]{4,3,2,1,0:T(8,128)S(1)}, bf16[2,2,256,256]{3,2,1,0:T(8,128)(2,1)S(1)}, bf16[4,256,256]{2,1,0:T(8,128)(2,1)S(1)}, f32[2,16,51...) custom-call(bf16[512,2048]{1,0:T(8,128)(2,1)} %bitcast.19, ...), custom_call_target="tpu_custom_call" | custom-call | tf_op jit(solution)/shard_map/pallas_call | solution.py:405
  5.5 0.0 copy-start
  5.6 17.9 %all_to_all.35 = f32[64,32,128]{2,1,0:T(8,128)S(1)} all-to-all(f32[64,32,128]{2,1,0:T(8,128)S(1)} %bitcast.18), channel_id=1, replica_groups=mesh['dp'=8,'zh'=8,'zl'=2,'axial'=4] {'zl','axial'}, dimensions={0} | all-to-all | bytes 2097152 | tf_op jit(solution)/shard_map/all_to_all | solution.py:440
  23.5 0.1 shard_map.101
  23.5 29.9 %all_to_all.36.refs_0_ = f32[8,32,128]{2,1,0:T(8,128)S(1)} all-to-all(f32[8,32,128]{2,1,0:T(8,128)S(1)} %shard_map.101), channel_id=1, replica_groups=mesh['dp'=8,'zh'=8,'zl'=2,'axial'=4] {'zh'}, dimensions={0} | all-to-all | bytes 262144 | tf_op jit(solution)/shard_map/all_to_all | solution.py:440
  53.4 0.0 copy-done
  53.4 0.7 shard_map.102
  54.2 15.7 %all_to_all.37 = f32[8,32,128]{2,1,0:T(8,128)S(1)} all-to-all(f32[8,32,128]{2,1,0:T(8,128)S(1)} %get-tuple-element.16), channel_id=1, replica_groups=mesh['dp'=8,'zh'=8,'zl'=2,'axial'=4] {'zh'}, dimensions={0} | all-to-all | bytes 262144 | tf_op jit(solution)/shard_map/all_to_all | solution.py:440
  69.9 0.1 broadcast_in_dim.10
  70.0 12.8 %all_to_all.38 = f32[64,32,128]{2,1,0:T(8,128)S(1)} all-to-all(f32[64,32,128]{2,1,0:T(8,128)S(1)} %bitcast.21), channel_id=1, replica_groups=mesh['dp'=8,'zh'=8,'zl'=2,'axial'=4] {'zl','axial'}, dimensions={0} | all-to-all | bytes 2097152 | tf_op jit(solution)/shard_map/all_to_all | solution.py:440
  82.9 9.8 %shard_map.103 = f32[2,4,8,32,128]{4,3,2,1,0:T(8,128)S(1)} custom-call(f32[2,4,8,32,128]{4,3,2,1,0:T(8,128)S(1)} %bitcast.13, bf16[2,2,256,256]{3,2,1,0:T(8,128)(2,1)S(1)} %get-tuple-element.17.halves, bf16[4,256,256]{2,1,0:T(8,128)(2,1)S(1)} %get-tuple-element.18.turn, f32[2,16,512]{2,1,0:T(8,128)S(1)} %get-tuple-element.19.place, ...), custom_call_target="tpu_custom_call" | custom-call | tf_op jit(solution)/shard_map/pallas_call | solution.py:405
  92.7 13.7 %all_to_all.39 = f32[64,32,128]{2,1,0:T(8,128)S(1)} all-to-all(f32[64,32,128]{2,1,0:T(8,128)S(1)} %bitcast.14), channel_id=1, replica_groups=mesh['dp'=8,'zh'=8,'zl'=2,'axial'=4] {'zl','axial'}, dimensions={0} | all-to-all | bytes 2097152 | tf_op jit(solution)/shard_map/all_to_all | solution.py:440
  106.4 0.1 shard_map.104
  106.4 15.6 %all_to_all.40.refs_0_ = f32[8,32,128]{2,1,0:T(8,128)S(1)} all-to-all(f32[8,32,128]{2,1,0:T(8,128)S(1)} %shard_map.104), channel_id=1, replica_groups=mesh['dp'=8,'zh'=8,'zl'=2,'axial'=4] {'zh'}, dimensions={0} | all-to-all | bytes 262144 | tf_op jit(solution)/shard_map/all_to_all | solution.py:440
  122.1 18.3 %all_to_all.41.pairs = f32[8,64,128]{2,1,0:T(8,128)S(1)} all-to-all(f32[8,64,128]{2,1,0:T(8,128)S(1)} %shard_map.105), channel_id=1, replica_groups=mesh['dp'=8,'zh'=8,'zl'=2,'axial'=4] {'dp'}, dimensions={0} | all-to-all | bytes 524288 | tf_op jit(solution)/shard_map/all_to_all | solution.py:511
  140.4 2.1 %shard_map.106 = f32[2,4,16,32,32]{4,3,2,1,0:T(8,128)} custom-call(f32[8,64,128]{2,1,0:T(8,128)S(1)} %all_to_all.41.pairs), custom_call_target="tpu_custom_call" | custom-call | tf_op jit(solution)/shard_map/pallas_call | solution.py:405
  (1 shorter events, 0.0 us)
Async XLA Ops:
  5.5 47.9 %copy-start = (bf16[2,1,4,16,32,32]{5,4,3,2,1,0:T(8,128)(2,1)S(1)}, bf16[2,1,4,16,32,32]{5,4,3,2,1,0:T(8,128)(2,1)}, u32[]{:S(2)}) copy-start(bf16[2,1,4,16,32,32]{5,4,3,2,1,0:T(8,128)(2,1)} %param.12) | copy-start | bytes 786436

commit v7 on v6

--- a/solution.py
+++ b/solution.py
@@ -27,13 +27,6 @@
 def split(values):
     high = values.astype(BF)
     return high, (values - high.astype(F32)).astype(BF)
-
-
-def split3(values):
-    high = values.astype(BF)
-    rest = values - high.astype(F32)
-    mid = rest.astype(BF)
-    return high, mid, (rest - mid.astype(F32)).astype(BF)
 
 
 def dot(a, b):
@@ -243,7 +236,8 @@
         copy.start()
     azimuth_synthesis(mixed, turn, place, synth)
     step = x.shape[1] // GROUPS
-    shift = jnp.concatenate([bias[...]] * (step // bias.shape[1]), 1)
+    lane = lax.broadcasted_iota(jnp.int32, (1, bias.shape[1]), 1)
+    synth[:, : bias.shape[1]] += jnp.where(lane == 0, bias[...], 0.0)
     slope = math.sqrt(2.0 / math.pi)
 
     half = synth.shape[1] // 2
@@ -262,7 +256,7 @@
 
     def activate(g):
         at = slice(g * step, (g + 1) * step)
-        value = pre[g] + dot(mix[...], x[:, at]) + shift
+        value = pre[g] + dot(mix[...], x[:, at])
         square = value * value
         t = jnp.tanh(value * (slope + (slope * 0.044715) * square))
         inner = value * (slope + (3.0 * slope * 0.044715) * square)
@@ -346,13 +340,13 @@
         total = total + parts[z]
     total = total * scale
     spec[...] = total
-    stack = jnp.concatenate([*split3(total[:n_kl]), *split3(total[n_kl:])], 0)
+    stack = jnp.concatenate([*split(total[:n_kl]), *split(total[n_kl:])], 0)
     row = lax.broadcasted_iota(jnp.int32, (stack.shape[0], 2 * lanes), 0) % n_kl
     got = jnp.zeros((stack.shape[0], 2 * lanes), F32)
     for kl in range(n_kl):
         got = jnp.where(row == kl, dot(stack, weight[kl]), got)
-    by_re = got[:n_kl] + got[n_kl : 2 * n_kl] + got[2 * n_kl : 3 * n_kl]
-    by_im = got[3 * n_kl : 4 * n_kl] + got[4 * n_kl : 5 * n_kl] + got[5 * n_kl :]
+    by_re = got[:n_kl] + got[n_kl : 2 * n_kl]
+    by_im = got[2 * n_kl : 3 * n_kl] + got[3 * n_kl :]
     re = (by_re[:, :lanes] - by_im[:, lanes:]) * out_scale
     im = (by_re[:, lanes:] + by_im[:, :lanes]) * out_scale
     for z in range(far):
@@ -516,7 +510,7 @@
         pairs,
         in_specs=[near_by],
         out_specs=far_off,
-        scratch_shapes=[pltpu.VMEM(grad_dims, F32), pltpu.SemaphoreType.DMA((4,))],
+        scratch_shapes=[pltpu.VMEM(grad_dims, F32), pltpu.SemaphoreType.DMA((8,))],
     )
     return grad[:, None]
 

time: 143 us -> 143 us (level)
  no operation moved by 1% of the time
where the time goes in v7:
time: 143 us; the launch traced here: 142 us
  blocking collectives  124 us (87%)
  Pallas kernels  18 us (13%)
    all_to_all x6, blocking collectives, exchange(): return lax.all_to_all(flat, axes, 0, 0, tiled=True).reshape(values.shape)  106 us
    all_to_all x1, blocking collectives, per_device(): pairs = lax.all_to_all(pairs, 'dp', 0, 0, tiled=True)  18.3 us
    pallas_call x7, Pallas kernels, call(): pl.pallas_call(kernel, out_shape=out_shape, compiler_params=pltpu.Compile...  18 us

profile of v7, /device:TPU:1, one launch (start us, length us, event | category | flops | bytes accessed | tf_op | source)
XLA Modules:
  0.0 142.3 jit_solution(3190339563774029581)
XLA Ops:
  0.0 5.5 %shard_map.100 = (f32[2,4,8,32,128]{4,3,2,1,0:T(8,128)S(1)}, bf16[2,2,256,256]{3,2,1,0:T(8,128)(2,1)S(1)}, bf16[4,256,256]{2,1,0:T(8,128)(2,1)S(1)}, f32[2,16,51...) custom-call(bf16[512,2048]{1,0:T(8,128)(2,1)} %bitcast.19, ...), custom_call_target="tpu_custom_call" | custom-call | tf_op jit(solution)/shard_map/pallas_call | solution.py:399
  5.5 0.0 copy-start
  5.6 17.9 %all_to_all.35 = f32[64,32,128]{2,1,0:T(8,128)S(1)} all-to-all(f32[64,32,128]{2,1,0:T(8,128)S(1)} %bitcast.18), channel_id=1, replica_groups=mesh['dp'=8,'zh'=8,'zl'=2,'axial'=4] {'zl','axial'}, dimensions={0} | all-to-all | bytes 2097152 | tf_op jit(solution)/shard_map/all_to_all | solution.py:434
  23.5 0.1 shard_map.101
  23.5 29.9 %all_to_all.36.refs_0_ = f32[8,32,128]{2,1,0:T(8,128)S(1)} all-to-all(f32[8,32,128]{2,1,0:T(8,128)S(1)} %shard_map.101), channel_id=1, replica_groups=mesh['dp'=8,'zh'=8,'zl'=2,'axial'=4] {'zh'}, dimensions={0} | all-to-all | bytes 262144 | tf_op jit(solution)/shard_map/all_to_all | solution.py:434
  53.4 0.0 copy-done
  53.4 0.6 shard_map.102
  54.1 15.7 %all_to_all.37 = f32[8,32,128]{2,1,0:T(8,128)S(1)} all-to-all(f32[8,32,128]{2,1,0:T(8,128)S(1)} %get-tuple-element.16), channel_id=1, replica_groups=mesh['dp'=8,'zh'=8,'zl'=2,'axial'=4] {'zh'}, dimensions={0} | all-to-all | bytes 262144 | tf_op jit(solution)/shard_map/all_to_all | solution.py:434
  69.8 0.1 broadcast_in_dim.10
  70.0 12.8 %all_to_all.38 = f32[64,32,128]{2,1,0:T(8,128)S(1)} all-to-all(f32[64,32,128]{2,1,0:T(8,128)S(1)} %bitcast.21), channel_id=1, replica_groups=mesh['dp'=8,'zh'=8,'zl'=2,'axial'=4] {'zl','axial'}, dimensions={0} | all-to-all | bytes 2097152 | tf_op jit(solution)/shard_map/all_to_all | solution.py:434
  82.8 9.7 %shard_map.103 = f32[2,4,8,32,128]{4,3,2,1,0:T(8,128)S(1)} custom-call(f32[2,4,8,32,128]{4,3,2,1,0:T(8,128)S(1)} %bitcast.13, bf16[2,2,256,256]{3,2,1,0:T(8,128)(2,1)S(1)} %get-tuple-element.17.halves, bf16[4,256,256]{2,1,0:T(8,128)(2,1)S(1)} %get-tuple-element.18.turn, f32[2,16,512]{2,1,0:T(8,128)S(1)} %get-tuple-element.19.place, ...), custom_call_target="tpu_custom_call" | custom-call | tf_op jit(solution)/shard_map/pallas_call | solution.py:399
  92.5 13.7 %all_to_all.39 = f32[64,32,128]{2,1,0:T(8,128)S(1)} all-to-all(f32[64,32,128]{2,1,0:T(8,128)S(1)} %bitcast.14), channel_id=1, replica_groups=mesh['dp'=8,'zh'=8,'zl'=2,'axial'=4] {'zl','axial'}, dimensions={0} | all-to-all | bytes 2097152 | tf_op jit(solution)/shard_map/all_to_all | solution.py:434
  106.1 0.1 shard_map.104
  106.2 15.6 %all_to_all.40.refs_0_ = f32[8,32,128]{2,1,0:T(8,128)S(1)} all-to-all(f32[8,32,128]{2,1,0:T(8,128)S(1)} %shard_map.104), channel_id=1, replica_groups=mesh['dp'=8,'zh'=8,'zl'=2,'axial'=4] {'zh'}, dimensions={0} | all-to-all | bytes 262144 | tf_op jit(solution)/shard_map/all_to_all | solution.py:434
  121.8 18.3 %all_to_all.41.pairs = f32[8,64,128]{2,1,0:T(8,128)S(1)} all-to-all(f32[8,64,128]{2,1,0:T(8,128)S(1)} %shard_map.105), channel_id=1, replica_groups=mesh['dp'=8,'zh'=8,'zl'=2,'axial'=4] {'dp'}, dimensions={0} | all-to-all | bytes 524288 | tf_op jit(solution)/shard_map/all_to_all | solution.py:505
  140.1 2.0 %shard_map.106 = f32[2,4,16,32,32]{4,3,2,1,0:T(8,128)} custom-call(f32[8,64,128]{2,1,0:T(8,128)S(1)} %all_to_all.41.pairs), custom_call_target="tpu_custom_call" | custom-call | tf_op jit(solution)/shard_map/pallas_call | solution.py:399
  (1 shorter events, 0.0 us)
Async XLA Ops:
  5.5 47.9 %copy-start = (bf16[2,1,4,16,32,32]{5,4,3,2,1,0:T(8,128)(2,1)S(1)}, bf16[2,1,4,16,32,32]{5,4,3,2,1,0:T(8,128)(2,1)}, u32[]{:S(2)}) copy-start(bf16[2,1,4,16,32,32]{5,4,3,2,1,0:T(8,128)(2,1)} %param.12) | copy-start | bytes 786436
